TPU v7x, 256 devices: a whole 4x4x8 slice. The times are simulated.
256 devices in a mesh: ab: 8 (over y, z_lo), cd: 32 (over z_hi, x, core).
Axes of the slice: x: 4, y: 4, z: 8 (z_hi: 4, z_lo: 2; z = z_hi * 2 + z_lo), core: 2. Of those that a mesh axis runs over, the one named last changes fastest.
Arguments:
- amplitudes: float32 [768, 16384], P('cd', 'ab'), may hold values from -1.25 to 1.25
- driver: float32 [768, 16384], P('cd', 'ab'), may hold values from -6 to 6
- ladder: bfloat16 [16384, 16384], P('ab', 'cd'), may hold values from -0.125 to 0.125
- block_mask: int32 [128, 128], P('ab', 'cd'), may hold values 0 or 1
- pair_list: int32 [768], replicated, may hold values from 0 to 1023, as said below
- occ_energy: float32 [32], replicated, may hold values from -2 to -0.5
- virt_energy: float32 [128], replicated, may hold values from 0.5 to 3
Outputs:
- new_amplitudes: float32 [768, 16384], P('cd', 'ab')
Inputs may be any that keep to these rules, and one draw needn't show every extreme that they name: `pair_list`: the entries are distinct occupied pairs i * 32 + j. Rows come in aligned blocks of two: a pair with i != j shares its block with the pair (j, i); pairs with i == j stand two to a block. Pairs 0 and 1023 are always listed.
All inputs are finite; a program needn't handle non-finite values. No bound on the sum of `block_mask` on one device may be relied on, other than what follows from the above.
Results may differ from a plain program's by a relative error of at most 0.008.
Values may be sent and summed in bfloat16 or wider, within the bound.
No kernel may reach another device: no remote copies, remote signals or barrier semaphores. Data moves between devices by JAX's collectives and lax.ppermute only.
A program may use at most 64 MiB of HBM per device.

v0:
```python
import jax
import jax.numpy as jnp
from jax import lax
from jax.sharding import PartitionSpec as P

NV = 128
NOCC = 32
BLK = 128
ITERS = 2


def swap_rows(values, diagonal_rows):
    row_count = values.shape[0]
    swapped = jnp.flip(values.reshape(row_count // 2, 2, -1), axis=1).reshape(row_count, -1)
    return jnp.where(diagonal_rows[:, None], values, swapped)


def body(amplitudes, driver, ladder, block_mask, pair_list, occ_energy, virt_energy):
    ab_count = lax.axis_size("ab")
    ab_index = lax.axis_index("ab")
    cd_index = lax.axis_index("cd")
    rows_dev, cols_dev = amplitudes.shape
    out_rows, in_cols = ladder.shape
    tile_width = NV // ab_count
    tile_area = tile_width * tile_width
    weights = ladder.reshape(out_rows // BLK, BLK, in_cols // BLK, BLK)
    weights = (weights * block_mask.astype(jnp.bfloat16)[:, None, :, None]).reshape(
        out_rows, in_cols
    )
    pairs_local = ab_index * cols_dev + jnp.arange(cols_dev, dtype=jnp.int32)
    big_a = pairs_local // (tile_width * NV)
    big_b = pairs_local // tile_area % ab_count
    first = big_a * tile_width + pairs_local // tile_width % tile_width
    second = big_b * tile_width + pairs_local % tile_width
    virt_index = jnp.arange(NV, dtype=jnp.int32)
    picks = (first[:, None] == virt_index).astype(jnp.float32) + (
        second[:, None] == virt_index
    ).astype(jnp.float32)
    col_energy = jnp.dot(picks, virt_energy, precision=lax.Precision.HIGHEST)
    row_pairs = lax.dynamic_slice_in_dim(pair_list, cd_index * rows_dev, rows_dev)
    occ_index = jnp.arange(NOCC, dtype=jnp.int32)
    occ_picks = (row_pairs[:, None] // NOCC == occ_index).astype(jnp.float32)
    occ_picks = occ_picks + (row_pairs[:, None] % NOCC == occ_index).astype(jnp.float32)
    row_energy = jnp.dot(occ_picks, occ_energy, precision=lax.Precision.HIGHEST)
    denominator = col_energy[None, :] - row_energy[:, None]
    all_diagonal = pair_list // NOCC == pair_list % NOCC
    turned_weights = jnp.swapaxes(
        weights.reshape(out_rows // tile_area, tile_width, tile_width, in_cols), 1, 2
    )
    turned_weights = turned_weights.reshape(out_rows, in_cols)
    state = amplitudes
    for step in range(ITERS):
        rounded = state.astype(jnp.bfloat16)
        regrouped = lax.all_to_all(rounded, "cd", split_axis=1, concat_axis=0, tiled=True)
        piece = lax.all_gather(regrouped, "ab", axis=1, tiled=True)
        flipped_piece = swap_rows(piece, all_diagonal)
        direct = lax.dot_general(
            piece, weights, (((1,), (1,)), ((), ())), preferred_element_type=jnp.float32
        )
        mirrored = lax.dot_general(
            flipped_piece,
            turned_weights,
            (((1,), (1,)), ((), ())),
            preferred_element_type=jnp.float32,
        )
        partial_value, mirrored = (direct, mirrored)
        partial_low = partial_value.astype(jnp.bfloat16)
        mirrored_low = mirrored.astype(jnp.bfloat16)
        tiles = lax.all_to_all(
            mirrored_low.reshape(partial_value.shape[0], ab_count, tile_area),
            "ab",
            split_axis=1,
            concat_axis=1,
            tiled=True,
        )
        combined = partial_low.astype(jnp.float32) + tiles.reshape(
            partial_value.shape[0], out_rows
        ).astype(jnp.float32)
        symmetric = lax.psum_scatter(
            combined.astype(jnp.bfloat16), "cd", scatter_dimension=0, tiled=True
        ).astype(jnp.float32)
        state = (driver + symmetric) / denominator
    return state


def solution(mesh):
    placed = (P("cd", "ab"), P("cd", "ab"), P("ab", "cd"), P("ab", "cd"), P(), P(), P())
    return jax.shard_map(body, mesh=mesh, in_specs=placed, out_specs=P("cd", "ab"), check_vma=False)
```

profile of v0, /device:TPU:2, one launch (start us, length us, event | category | flops | bytes accessed | tf_op | source)
XLA Modules:
  0.0 419.7 jit_solution(11459490337103012838)
XLA Ops:
  6.5 1.0 convert_element_type.68
  7.8 0.8 reshape.166
  8.6 11.6 %all-to-all-start = ((bf16[32,2,768]{2,1,0:T(2,128)(2,1)}), bf16[32,2,768]{2,1,0:T(2,128)(2,1)S(1)}, u32[]{:S(2)}, u32[]{:S(2)}) async-start(bf16[32,2,768]{2,1,0:T(2,128)(2,1)} %reshape.166), calls=%async_computation | async-start | bytes 196608 | tf_op jit(solution)/shard_map/all_to_all | solution.py:54
  20.2 0.7 convert_element_type.67
  21.2 1.8 multiply_bitcast_fusion
  23.0 2.6 copy.89
  25.6 3.7 all-to-all-done
  29.6 31.5 %all_gather.6 = bf16[768,512]{0,1:T(8,128)(2,1)S(1)} all-gather(bf16[768,64]{0,1:T(8,128)(2,1)S(1)} %copy.85), channel_id=1, replica_groups=mesh['ab'=8,'cd'=32] {'ab'}, dimensions={1}, use_global_device_ids=true | all-gather | bytes 884736 | tf_op jit(solution)/shard_map/all_gather | solution.py:55
  61.7 4.1 rev.7
  66.2 5.1 %convolution_convert_fusion.2 = bf16[768,2048]{1,0:T(8,128)(2,1)} fusion(bf16[2048,512]{1,0:T(8,128)(2,1)} %bitcast.60, bf16[768,512]{1,0:T(8,128)(2,1)S(1)} %copy.87, bf16[768,512]{1,0:T(8,128)(2,1)S(1)} %reshape.149, pred[768]{0:T(1024)(128)(4,1)S(1)} %fusion.31), kind=kOutput, calls=%fused_computation.6 | convolution fusion | flops 1612578816 | bytes 6816512 | tf_op jit(solution)/shard_map/dot_general | solution.py:60
  71.3 3.2 copy.100
  74.5 37.8 %all_to_all.48 = bf16[768,8,256]{0,2,1:T(8,128)(2,1)S(1)} all-to-all(bf16[768,8,256]{0,2,1:T(8,128)(2,1)S(1)} %bitcast.54), channel_id=1, replica_groups=mesh['ab'=8,'cd'=32] {'ab'}, dimensions={1} | all-to-all | bytes 6291456 | tf_op jit(solution)/shard_map/all_to_all | solution.py:69
  112.2 0.6 mul.40
  112.9 3.7 fusion
  116.5 4.7 %copy.101 = bf16[768,2048]{1,0:T(8,128)(2,1)} copy(bf16[768,2048]{0,1:T(8,128)(2,1)} %fusion) | data formatting | bytes 6291456
  122.1 1.6 fusion.1
  123.7 87.4 %reduce-scatter.7.cloned.1.call-done = bf16[24,2048]{1,0:T(8,128)(2,1)} async-done(((bf16[768,2048]{1,0:T(8,128)(2,1)}), bf16[24,2048]{1,0:T(8,128)(2,1)}) %reduce-scatter.7.cloned.1.call-update) | async-done | bytes 98320 | tf_op jit(solution)/shard_map/reduce_scatter | solution.py:79
  211.1 1.0 fusion.11
  212.5 16.2 %all_to_all.49 = bf16[32,2,768]{2,1,0:T(2,128)(2,1)S(1)} all-to-all(bf16[32,2,768]{2,1,0:T(2,128)(2,1)S(1)} %reshape.168), channel_id=1, replica_groups=mesh['ab'=8,'cd'=32] {'cd'}, dimensions={0} | all-to-all | bytes 196608 | tf_op jit(solution)/shard_map/all_to_all | solution.py:54
  229.1 31.4 %all_gather.7 = bf16[768,512]{0,1:T(8,128)(2,1)S(1)} all-gather(bf16[768,64]{0,1:T(8,128)(2,1)S(1)} %copy.93), channel_id=1, replica_groups=mesh['ab'=8,'cd'=32] {'ab'}, dimensions={1}, use_global_device_ids=true | all-gather | bytes 884736 | tf_op jit(solution)/shard_map/all_gather | solution.py:55
  260.5 1.2 copy.95
  261.7 2.8 reshape.153
  264.5 8.0 %rev.8 = bf16[384,2,512]{2,1,0:T(2,128)(2,1)} reverse(bf16[384,2,512]{2,1,0:T(2,128)(2,1)} %reshape.153), dimensions={1} | reverse | bytes 1572864 | tf_op jit(solution)/shard_map/jit(_flip)/rev | solution.py:14
  272.5 3.0 reshape.154
  275.4 3.9 convolution_convert_fusion
  279.6 37.5 %all_to_all.50 = bf16[768,8,256]{2,0,1:T(8,128)(2,1)S(1)} all-to-all(bf16[768,8,256]{2,0,1:T(8,128)(2,1)S(1)} %bitcast.55), channel_id=1, replica_groups=mesh['ab'=8,'cd'=32] {'ab'}, dimensions={1} | all-to-all | bytes 6291456 | tf_op jit(solution)/shard_map/all_to_all | solution.py:69
  317.1 0.6 convert_bitcast_fusion
  317.6 0.9 copy.106
  318.6 0.6 copy-done.2
  319.2 3.6 add_convert_fusion
  322.8 88.4 %reduce-scatter.9.cloned.1.call-done = bf16[24,2048]{1,0:T(8,128)(2,1)} async-done(((bf16[768,2048]{1,0:T(8,128)(2,1)}), bf16[24,2048]{1,0:T(8,128)(2,1)}) %reduce-scatter.9.cloned.1.call-update) | async-done | bytes 98320 | tf_op jit(solution)/shard_map/reduce_scatter | solution.py:79
  411.2 1.7 subtract_divide_fusion
  (39 shorter events, 3.5 us)
Async XLA Ops:
  6.5 115.5 %copy-start = (f32[128]{0:T(128)S(1)}, f32[128]{0:T(128)}, u32[]{:S(2)}) copy-start(f32[128]{0:T(128)} %param.13) | copy-start | bytes 1540
  8.6 20.7 %all-to-all-start = ((bf16[32,2,768]{2,1,0:T(2,128)(2,1)}), bf16[32,2,768]{2,1,0:T(2,128)(2,1)S(1)}, u32[]{:S(2)}, u32[]{:S(2)}) async-start(bf16[32,2,768]{2,1,0:T(2,128)(2,1)} %reshape.166), calls=%async_computation | async-start | bytes 196608 | tf_op jit(solution)/shard_map/all_to_all | solution.py:54
  20.2 190.9 %reduce-scatter.7.cloned.1.call-start = ((), (), s32[]{:S(2)}) async-start(), calls=%async_computation.6 | async-start | bytes 3244032 | tf_op jit(solution)/shard_map/reduce_scatter | solution.py:79
  23.0 2.6 copy-start.6
  61.1 5.1 %copy-start.3 = (bf16[768,512]{0,1:T(8,128)(2,1)}, bf16[768,512]{0,1:T(8,128)(2,1)S(1)}, u32[]{:S(2)}) copy-start(bf16[768,512]{0,1:T(8,128)(2,1)S(1)} %all_gather.6) | copy-start | bytes 2359300
  74.5 38.4 %copy-start.1 = (bf16[2048,512]{1,0:T(8,128)(2,1)S(1)}, bf16[2048,512]{1,0:T(8,128)(2,1)}, u32[]{:S(2)}) copy-start(bf16[2048,512]{1,0:T(8,128)(2,1)} %param.9) | copy-start | bytes 6291460
  74.5 38.4 %copy-start.4 = (bf16[768,512]{0,1:T(8,128)(2,1)S(1)}, bf16[768,512]{0,1:T(8,128)(2,1)}, u32[]{:S(2)}) copy-start(bf16[768,512]{0,1:T(8,128)(2,1)} %copy-done.3) | copy-start | bytes 2359300
  121.2 0.7 copy-start.7
  121.2 89.9 %copy-start.5 = (f32[24,2048]{1,0:T(8,128)S(1)}, f32[24,2048]{1,0:T(8,128)}, u32[]{:S(2)}) copy-start(f32[24,2048]{1,0:T(8,128)} %param.8) | copy-start | bytes 589828
  121.2 290.0 %reduce-scatter.9.cloned.1.call-start = ((), (), s32[]{:S(2)}) async-start(), calls=%async_computation.7 | async-start | bytes 3244032 | tf_op jit(solution)/shard_map/reduce_scatter | solution.py:79
  317.6 1.6 copy-start.2
Sparse Core Ops, SparseCore 0:
  121.4 89.6 reduce-scatter.6
  322.9 88.2 reduce-scatter.8
where the time goes:
time: 422 us; the launch traced here: 420 us
  waiting for transfers between devices  180 us (43%)
  blocking collectives  154 us (36%)
  local copies, waits for them, and re-layouts  35.6 us (8%)
  matrix products  18 us (4%)
  between operations  13.7 us (3%)
  starting transfers between devices  11.7 us (3%)
  other arithmetic  6.8 us (2%)
    reduce_scatter x2, waiting for transfers between devices, body(): lax.psum_scatter(combined.astype(jnp.bfloat16), 'cd', scatter_dimension=0...  176 us
    all_to_all x2, blocking collectives, body(): lax.all_to_all(mirrored_low.reshape(partial_value.shape[0], ab_count, til...  75.2 us
    all_gather x2, blocking collectives, body(): piece = lax.all_gather(regrouped, 'ab', axis=1, tiled=True)  62.9 us
    all_to_all x1, blocking collectives, body(): lax.all_to_all(rounded, 'cd', split_axis=1, concat_axis=0, tiled=True)  16.2 us
    rev x2, local copies, waits for them, and re-layouts, swap_rows(): jnp.flip(values.reshape(row_count // 2, 2, -1), axis=1)  12.1 us
    all_to_all x1, starting transfers between devices, body(): lax.all_to_all(rounded, 'cd', split_axis=1, concat_axis=0, tiled=True)  11.6 us
    dot_general x2, matrix products, body(): lax.dot_general(flipped_piece, turned_weights, (((1,), (1,)), ((), ())),...  9 us
  transfers between devices with their start and end apart: 3, of which 3 were waited for; matrix products, arithmetic and copies ran while one was open for 2% of the time, Pallas kernels for 0%

commit v1 on v0

v1 whole, which is shorter than its diff:
```python
import jax
import jax.numpy as jnp
import numpy as np
from jax import lax
from jax.experimental import pallas as pl
from jax.experimental.pallas import tpu as pltpu
from jax.sharding import Mesh, PartitionSpec as P

NV = 128
NOCC = 32
BLK = 128
BF = jnp.bfloat16
F32 = jnp.float32
AB = ("y", "zl")
GRID = ("x", "zh")
ALL = ("y", "zl", "zh", "x", "core")
VMEM = pl.BlockSpec(memory_space=pltpu.VMEM)
SMEM = pl.BlockSpec(memory_space=pltpu.SMEM)
LIMIT = 48 * 1024 * 1024


def call(kernel, out_shape, inputs, scalars=0, scratch=()):
    specs = [SMEM] * scalars + [VMEM] * (len(inputs) - scalars)
    outs = jax.tree.map(lambda _: VMEM, out_shape)
    return pl.pallas_call(
        kernel,
        out_shape=out_shape,
        in_specs=specs,
        out_specs=outs,
        scratch_shapes=list(scratch),
        compiler_params=pltpu.CompilerParams(vmem_limit_bytes=LIMIT),
    )(*inputs)


def weave_kernel(core_ref, own_ref, other_ref, out_ref):
    first = core_ref[0] == 0
    rows = 256

    def step(i, carry):
        here = pl.ds(pl.multiple_of(i * rows, rows), rows)
        for t in range(own_ref.shape[1] // BLK):
            mine = own_ref[here, t * BLK : (t + 1) * BLK]
            theirs = other_ref[here, t * BLK : (t + 1) * BLK]
            a = jnp.where(first, mine, theirs)
            b = jnp.where(first, theirs, mine)
            half = BLK // 2
            out_ref[here, 2 * t * BLK : (2 * t + 1) * BLK] = jnp.concatenate(
                [a[:, :half], b[:, :half]], axis=1
            )
            out_ref[here, (2 * t + 1) * BLK : (2 * t + 2) * BLK] = jnp.concatenate(
                [a[:, half:], b[:, half:]], axis=1
            )
        return carry

    lax.fori_loop(0, own_ref.shape[0] // rows, step, 0)


def product(low_ref, w_ref, n, width):
    low = jnp.concatenate([low_ref[s] for s in range(low_ref.shape[0])], axis=1)
    w = w_ref[n * width : (n + 1) * width, :]
    return lax.dot_general(low, w, (((1,), (1,)), ((), ())), preferred_element_type=F32)


def columns_kernel(low_ref, w_ref, out_ref):
    n_x = out_ref.shape[0]
    width = 256
    for n in range(w_ref.shape[0] // width):
        part = product(low_ref, w_ref, n, width).astype(BF)
        for j in range(width // BLK):
            q = n * (width // BLK) + j
            out_ref[q % n_x, q // n_x] = part[:, j * BLK : (j + 1) * BLK]


def rows_kernel(low_ref, w_ref, out_ref):
    n_x, rows, _ = out_ref.shape
    width = 256
    for n in range(w_ref.shape[0] // width):
        part = product(low_ref, w_ref, n, width).astype(BF)
        for j in range(n_x):
            out_ref[j, :, n * width : (n + 1) * width] = part[j * rows : (j + 1) * rows]


def sum_leading(ref):
    total = ref[0].astype(F32)
    for i in range(1, ref.shape[0]):
        total = total + ref[i].astype(F32)
    return total


def sum_kernel(pieces_ref, total_ref, low_ref):
    total = sum_leading(pieces_ref)
    total_ref[...] = total
    low_ref[...] = total.astype(BF)


def swap_rows(values, diagonal):
    rows = values.shape[0]
    up = pltpu.roll(values, rows - 1, 0)
    down = pltpu.roll(values, 1, 0)
    even = lax.broadcasted_iota(jnp.int32, values.shape, 0) % 2 == 0
    return jnp.where(diagonal != 0, values, jnp.where(even, up, down))


def close_columns_kernel(half_ref, total_ref, same_ref, cross_ref, drv_ref, den_ref, diag_ref, out_ref):
    half = half_ref[0]
    lane_in = lax.broadcasted_iota(jnp.int32, (BLK, BLK), 0)
    lane_out = lax.broadcasted_iota(jnp.int32, (BLK, BLK), 1)
    goes = lane_in % 16 == half * 8 + lane_out // 16
    yy = lane_out % 16
    same = (goes & (yy == half * 8 + lane_in // 16)).astype(F32).astype(BF)
    cross = (goes & (yy == (1 - half) * 8 + lane_in // 16)).astype(F32).astype(BF)
    mirrored = jnp.dot(same_ref[...], same, preferred_element_type=F32)
    mirrored = mirrored + jnp.dot(cross_ref[...], cross, preferred_element_type=F32)
    mirrored = swap_rows(mirrored, diag_ref[...])
    driver = drv_ref[0].astype(F32) + drv_ref[1].astype(F32)
    low = ((driver + (total_ref[...] + mirrored)) / den_ref[...]).astype(BF)
    for i in range(out_ref.shape[0]):
        out_ref[i] = low


def turn_kernel(pieces_ref, total_ref, out_ref):
    total = sum_leading(pieces_ref)
    total_ref[...] = total
    area = out_ref.shape[2]
    side = 16
    lane_in = lax.broadcasted_iota(jnp.int32, (area, area), 0)
    lane_out = lax.broadcasted_iota(jnp.int32, (area, area), 1)
    turn = (lane_in % side == lane_out // side) & (lane_in // side == lane_out % side)
    turn = turn.astype(F32).astype(BF)
    for b in range(out_ref.shape[0]):
        tile = total[:, b * area : (b + 1) * area].astype(BF)
        out_ref[b] = jnp.dot(tile, turn, preferred_element_type=F32).astype(BF)


def close_rows_kernel(total_ref, tiles_ref, driver_ref, row_ref, col_ref, diag_ref, out_ref):
    area = tiles_ref.shape[2]
    for b in range(tiles_ref.shape[0]):
        here = slice(b * area, (b + 1) * area)
        mirrored = swap_rows(tiles_ref[b].astype(F32), diag_ref[...])
        den = col_ref[:, here] - row_ref[...]
        out_ref[:, here] = (driver_ref[:, here] + (total_ref[:, here] + mirrored)) / den


def pick(table, index):
    hit = index[:, None] == jnp.arange(table.shape[0], dtype=jnp.int32)[None, :]
    return jnp.sum(jnp.where(hit, table[None, :], 0.0), axis=1)


def body(amplitudes, driver, ladder, block_mask, pair_list, occ_energy, virt_energy):
    n_x, n_zh, n_core = lax.axis_size("x"), lax.axis_size("zh"), lax.axis_size("core")
    n_ab = lax.axis_size(AB)
    cells = n_x * n_zh
    core, ix, izh = lax.axis_index("core"), lax.axis_index("x"), lax.axis_index("zh")
    ab_index = lax.axis_index(AB)
    rows, cols = amplitudes.shape
    out_rows, in_cols = ladder.shape
    wide = cols // cells
    many = rows * cells
    side = NV // n_ab
    area = side * side

    def cut(values):
        values = values.reshape(rows, n_zh, n_x, wide)
        return jnp.transpose(values, (2, 1, 0, 3)).reshape(cells, rows, wide)

    masked = ladder.reshape(out_rows // BLK, BLK, in_cols // BLK, BLK)
    masked = (masked * block_mask.astype(BF)[:, None, :, None]).reshape(out_rows, in_cols)
    other = lax.ppermute(masked, "core", [(0, 1), (1, 0)])

    high = lax.reduce_precision(driver, 8, 7)
    pack = jnp.concatenate(
        [cut(amplitudes.astype(BF)), cut(high.astype(BF)), cut((driver - high).astype(BF))], axis=2
    )
    pack = lax.all_to_all(pack, GRID, 0, 0, tiled=True).reshape(many, 3, wide)
    start = pack[:, 0]
    drv = jnp.stack([pack[:, 1], pack[:, 2]])

    weights = call(
        weave_kernel,
        jax.ShapeDtypeStruct((out_rows, 2 * in_cols), BF),
        [core.astype(jnp.int32).reshape(1), masked, other],
        1,
    )

    local = lax.dynamic_index_in_dim(
        pair_list.reshape(n_zh, n_x, n_core, rows), core, 2, keepdims=False
    )
    local = jnp.transpose(local, (1, 0, 2)).reshape(many)
    row_energy = pick(occ_energy, local // NOCC) + pick(occ_energy, local % NOCC)
    diag = (local // NOCC == local % NOCC).astype(jnp.int32)
    pairs = ab_index * cols + jnp.arange(cols, dtype=jnp.int32)
    first = pairs // (side * NV) * side + pairs // side % side
    second = pairs // area % n_ab * side + pairs % side
    col_energy = pick(virt_energy, first) + pick(virt_energy, second)
    cell = izh * n_x + ix
    here = lax.dynamic_slice_in_dim(col_energy, cell * wide, wide)
    den = here[None, :] - row_energy[:, None]
    mine = (ix * n_zh + izh) * rows
    my_rows = lax.dynamic_slice_in_dim(row_energy, mine, rows)
    my_diag = lax.dynamic_slice_in_dim(diag, mine, rows)

    def place(a, q, c):
        return ((a * (n_zh * n_x)) + q) * n_core + c

    same, cross = [], []
    for a in range(n_ab):
        for q in range(cells):
            for c in range(n_core):
                b, h = q // 2, q % 2
                same.append((place(a, q, c), place(b, 2 * a + h, c)))
                cross.append((place(a, q, c), place(b, 2 * a + 1 - h, c)))

    low = lax.all_to_all(jnp.broadcast_to(start[None], (n_ab, many, wide)), AB, 0, 0, tiled=True)
    part = call(columns_kernel, jax.ShapeDtypeStruct((n_x, n_zh, many, wide), BF), [low, weights])
    part = lax.all_to_all(part, "x", 0, 0, tiled=True)
    part = jnp.sum(part.astype(F32), axis=0).astype(BF)
    part = lax.all_to_all(part, "zh", 0, 0, tiled=True)
    total, rounded = call(
        sum_kernel,
        (jax.ShapeDtypeStruct((many, wide), F32), jax.ShapeDtypeStruct((many, wide), BF)),
        [part],
    )
    from_same = lax.ppermute(rounded, ALL, same)
    from_cross = lax.ppermute(rounded, ALL, cross)
    low = call(
        close_columns_kernel,
        jax.ShapeDtypeStruct((n_ab, many, wide), BF),
        [(cell % 2).astype(jnp.int32).reshape(1), total, from_same, from_cross, drv, den, diag[:, None]],
        1,
    )

    low = lax.all_to_all(low, AB, 0, 0, tiled=True)
    part = call(rows_kernel, jax.ShapeDtypeStruct((n_x, many // n_x, cols), BF), [low, weights])
    part = lax.all_to_all(part, "x", 0, 0, tiled=True)
    part = jnp.sum(part.astype(F32), axis=0).astype(BF).reshape(n_zh, rows, cols)
    part = lax.all_to_all(part, "zh", 0, 0, tiled=True)
    total, turned = call(
        turn_kernel,
        (jax.ShapeDtypeStruct((rows, cols), F32), jax.ShapeDtypeStruct((n_ab, rows, area), BF)),
        [part],
    )
    tiles = lax.all_to_all(turned, AB, 0, 0, tiled=True)
    return call(
        close_rows_kernel,
        jax.ShapeDtypeStruct((rows, cols), F32),
        [total, tiles, driver, my_rows[:, None], col_energy[None, :], my_diag[:, None]],
    )


def solution(mesh):
    fine = Mesh(mesh.devices.reshape(4, 2, 4, 4, 2), ALL)
    ab, cd = AB, ("zh", "x", "core")
    placed = (P(cd, ab), P(cd, ab), P(ab, cd), P(ab, cd), P(), P(), P())
    return jax.shard_map(body, mesh=fine, in_specs=placed, out_specs=P(cd, ab), check_vma=False)
```

time: 422 us -> 181 us (0.43)
  blocking collectives: 154 us -> 39.8 us
  waiting for transfers between devices: 180 us -> 72.2 us
  local copies, waits for them, and re-layouts: 35.6 us -> 3.24 us
  starting transfers between devices: 11.7 us -> 39.5 us
  matrix products: 18 us -> 0 us
  Pallas kernels: 0 us -> 16.7 us
  between operations: 13.7 us -> 0.29 us
    reduce_scatter x2 -> x0, waiting for transfers between devices: 176 us -> none  [body(): lax.psum_scatter(combined.astype(jnp.bfloat16), 'cd', scatter_dimension=0...]
    all_gather x2 -> x0, blocking collectives: 62.9 us -> none  [body(): piece = lax.all_gather(regrouped, 'ab', axis=1, tiled=True)]
    all_to_all x1 -> x6, waiting for transfers between devices: 3.73 us -> 58.3 us  [the longest x2 21.9 us: body(): part = lax.all_to_all(part, 'zh', 0, 0, tiled=True)]
    all_to_all x3 -> x2, blocking collectives: 91.5 us -> 39.8 us  [the longest x1 22.3 us: body(): part = lax.all_to_all(part, 'x', 0, 0, tiled=True)]
    all_to_all x1 -> x6, starting transfers between devices: 11.6 us -> 37.2 us  [the longest x1 11.5 us: body(): pack = lax.all_to_all(pack, GRID, 0, 0, tiled=True).reshape(many, 3, wide)]
    dot_general x6 -> x0, matrix products: 18 us -> none  [the longest x2 9 us: body(): lax.dot_general(flipped_piece, turned_weights, (((1,), (1,)), ((), ())),...]
    pallas_call x0 -> x7, Pallas kernels: none -> 16.7 us  [call(): pl.pallas_call(kernel, out_shape=out_shape, in_specs=specs, out_specs=out...]
    ppermute x0 -> x3, waiting for transfers between devices: none -> 13.9 us  [the longest x1 13.9 us: body(): from_cross = lax.ppermute(rounded, ALL, cross)]
  transfers between devices with their start and end apart: 3 -> 9, of which waited for: 3 -> 7; matrix products, arithmetic and copies ran while one was open for 2% -> 4% of each run, Pallas kernels for 0% -> 3%
where the time goes in v1:
time: 181 us; the launch traced here: 180 us
  waiting for transfers between devices  72.2 us (40%)
  blocking collectives  39.8 us (22%)
  starting transfers between devices  39.5 us (22%)
  Pallas kernels  16.7 us (9%)
  other arithmetic  8.49 us (5%)
  local copies, waits for them, and re-layouts  3.24 us (2%)
    all_to_all x1, blocking collectives, body(): part = lax.all_to_all(part, 'x', 0, 0, tiled=True)  22.3 us
    all_to_all x2, waiting for transfers between devices, body(): part = lax.all_to_all(part, 'zh', 0, 0, tiled=True)  21.9 us
    all_to_all x1, blocking collectives, body(): low = lax.all_to_all(low, AB, 0, 0, tiled=True)  17.5 us
    pallas_call x7, Pallas kernels, call(): pl.pallas_call(kernel, out_shape=out_shape, in_specs=specs, out_specs=out...  16.7 us
    all_to_all x1, waiting for transfers between devices, body(): part = lax.all_to_all(part, 'x', 0, 0, tiled=True)  15.2 us
    ppermute x1, waiting for transfers between devices, body(): from_cross = lax.ppermute(rounded, ALL, cross)  13.9 us
    all_to_all x1, starting transfers between devices, body(): pack = lax.all_to_all(pack, GRID, 0, 0, tiled=True).reshape(many, 3, wide)  11.5 us
    all_to_all x2, starting transfers between devices, body(): part = lax.all_to_all(part, 'zh', 0, 0, tiled=True)  11.2 us
  transfers between devices with their start and end apart: 9, of which 7 were waited for; matrix products, arithmetic and copies ran while one was open for 4% of the time, Pallas kernels for 3%

profile of v1, /device:TPU:2, one launch (start us, length us, event | category | flops | bytes accessed | tf_op | source)
XLA Modules:
  0.0 180.2 jit_solution(12569062387219947879)
XLA Ops:
  0.0 1.0 reduce-precision_convert_fusion
  1.1 0.9 convert_element_type.28
  2.2 0.7 pad_maximum_fusion
  2.9 11.5 %all-to-all-start = ((bf16[16,24,384]{2,1,0:T(8,128)(2,1)}), bf16[16,24,384]{2,1,0:T(8,128)(2,1)S(1)}, u32[]{:S(2)}, u32[]{:S(2)}) async-start(bf16[16,24,384]{2,1,0:T(8,128)(2,1)} %pad_maximum_fusion), calls=%async_computation | async-start | bytes 589824 | tf_op jit(solution)/shard_map/all_to_all | solution.py:174
  14.5 0.6 mul.44
  15.1 1.9 %bitcast_multiply_fusion.own_ref = bf16[2048,512]{1,0:T(8,128)(2,1)S(1)} fusion(bf16[2048,512]{1,0:T(8,128)(2,1)} %param.9, bf16[256,8,4,128]{3,2,1,0:T(4,128)(2,1)S(1)} %bitcast.29), kind=kLoop, calls=%fused_computation | loop fusion | flops 1048576 | bytes 6291456 | tf_op jit(solution)/shard_map/mul | solution.py:167
  17.1 9.0 %all-to-all-done = bf16[16,24,384]{2,1,0:T(8,128)(2,1)S(1)} async-done(((bf16[16,24,384]{2,1,0:T(8,128)(2,1)}), bf16[16,24,384]{2,1,0:T(8,128)(2,1)S(1)}, u32[]{:S(2)}, u32[]{:S(2)}) %all-to-all-start) | async-done | bytes 294944 | tf_op jit(solution)/shard_map/all_to_all | solution.py:174
  26.2 0.4 fusion.22
  26.7 1.0 broadcast_in_dim.63
  27.7 4.9 %all-to-all-start.1 = ((bf16[8,384,128]{2,1,0:T(8,128)(2,1)}), bf16[8,384,128]{2,1,0:T(8,128)(2,1)S(1)}, u32[]{:S(2)}, u32[]{:S(2)}) async-start(bf16[8,384,128]{2,1,0:T(8,128)(2,1)} %broadcast_in_dim.63), calls=%async_computation.1 | async-start | bytes 1572864 | tf_op jit(solution)/shard_map/all_to_all | solution.py:213
  32.6 5.5 %shard_map.73.w_ref = bf16[2048,1024]{1,0:T(8,128)(2,1)} custom-call(s32[1]{0:T(128)} %bitcast.7.core_ref, bf16[2048,512]{1,0:T(8,128)(2,1)S(1)} %bitcast_multiply_fusion.own_ref, bf16[2048,512]{1,0:T(8,128)(2,1)} %collective-permute-done.other_ref), custom_call_target="tpu_custom_call" | custom-call | tf_op jit(solution)/shard_map/pallas_call | solution.py:25
  38.1 6.0 %all-to-all-done.1.low_ref = bf16[8,384,128]{2,1,0:T(8,128)(2,1)S(1)} async-done(((bf16[8,384,128]{2,1,0:T(8,128)(2,1)}), bf16[8,384,128]{2,1,0:T(8,128)(2,1)S(1)}, u32[]{:S(2)}, u32[]{:S(2)}) %all-to-all-start.1) | async-done | bytes 786464 | tf_op jit(solution)/shard_map/all_to_all | solution.py:213
  44.1 5.2 %shard_map.74 = bf16[4,4,384,128]{3,2,1,0:T(8,128)(2,1)} custom-call(bf16[8,384,128]{2,1,0:T(8,128)(2,1)S(1)} %all-to-all-done.1.low_ref, bf16[2048,1024]{1,0:T(8,128)(2,1)} %shard_map.73.w_ref), custom_call_target="tpu_custom_call" | custom-call | tf_op jit(solution)/shard_map/pallas_call | solution.py:25
  49.3 6.2 %all-to-all-start.2 = ((bf16[4,4,384,128]{3,2,1,0:T(8,128)(2,1)}), bf16[4,4,384,128]{3,2,1,0:T(8,128)(2,1)S(1)}, u32[]{:S(2)}, u32[]{:S(2)}) async-start(bf16[4,4,384,128]{3,2,1,0:T(8,128)(2,1)} %shard_map.74), calls=%async_computation.2 | async-start | bytes 3145728 | tf_op jit(solution)/shard_map/all_to_all | solution.py:215
  56.1 1.3 select_reduce_fusion
  57.5 15.2 %all-to-all-done.2 = bf16[4,4,384,128]{3,2,1,0:T(8,128)(2,1)S(1)} async-done(((bf16[4,4,384,128]{3,2,1,0:T(8,128)(2,1)}), bf16[4,4,384,128]{3,2,1,0:T(8,128)(2,1)S(1)}, u32[]{:S(2)}, u32[]{:S(2)}) %all-to-all-start.2) | async-done | bytes 1572896 | tf_op jit(solution)/shard_map/all_to_all | solution.py:215
  72.6 1.1 reduce_sum.60
  73.7 3.5 %all-to-all-start.3 = ((bf16[4,384,128]{2,1,0:T(8,128)(2,1)}), bf16[4,384,128]{2,1,0:T(8,128)(2,1)S(1)}, u32[]{:S(2)}, u32[]{:S(2)}) async-start(bf16[4,384,128]{2,1,0:T(8,128)(2,1)} %reduce_sum.60), calls=%async_computation.3 | async-start | bytes 786432 | tf_op jit(solution)/shard_map/all_to_all | solution.py:217
  77.6 9.9 %all-to-all-done.3.pieces_ref = bf16[4,384,128]{2,1,0:T(8,128)(2,1)S(1)} async-done(((bf16[4,384,128]{2,1,0:T(8,128)(2,1)}), bf16[4,384,128]{2,1,0:T(8,128)(2,1)S(1)}, u32[]{:S(2)}, u32[]{:S(2)}) %all-to-all-start.3) | async-done | bytes 393248 | tf_op jit(solution)/shard_map/all_to_all | solution.py:217
  87.5 0.7 collective-permute-start.1
  88.1 1.5 collective-permute-start.2
  89.7 13.9 %collective-permute-done.2.cross_ref = bf16[384,128]{1,0:T(8,128)(2,1)S(1)} collective-permute-done((bf16[384,128]{1,0:T(8,128)(2,1)S(1)}, bf16[384,128]{1,0:T(8,128)(2,1)S(1)}, u32[]{:S(2)}, u32[]{:S(2)}) %collective-permute-start.2) | collective-permute-done | bytes 98336 | tf_op jit(solution)/shard_map/ppermute | solution.py:224
  103.9 17.5 %all_to_all.40.low_ref = bf16[8,384,128]{2,1,0:T(8,128)(2,1)S(1)} all-to-all(bf16[8,384,128]{2,1,0:T(8,128)(2,1)S(1)} %shard_map.76), channel_id=1, replica_groups=mesh['y'=4,'zl'=2,'zh'=4,'x'=4,'core'=2] {'y','zl'}, dimensions={0} | all-to-all | bytes 1572864 | tf_op jit(solution)/shard_map/all_to_all | solution.py:232
  121.4 4.0 %shard_map.77 = bf16[4,96,2048]{2,1,0:T(8,128)(2,1)S(1)} custom-call(bf16[8,384,128]{2,1,0:T(8,128)(2,1)S(1)} %all_to_all.40.low_ref, bf16[2048,1024]{1,0:T(8,128)(2,1)} %shard_map.73.w_ref), custom_call_target="tpu_custom_call" | custom-call | tf_op jit(solution)/shard_map/pallas_call | solution.py:25
  125.4 22.3 %all_to_all.41 = bf16[4,96,2048]{2,1,0:T(8,128)(2,1)S(1)} all-to-all(bf16[4,96,2048]{2,1,0:T(8,128)(2,1)S(1)} %shard_map.77), channel_id=1, replica_groups=mesh['y'=4,'zl'=2,'zh'=4,'x'=4,'core'=2] {'x'}, dimensions={0} | all-to-all | bytes 3145728 | tf_op jit(solution)/shard_map/all_to_all | solution.py:234
  147.7 1.1 reduce_sum.65
  148.8 7.7 %all-to-all-start.6 = ((bf16[4,24,2048]{2,1,0:T(8,128)(2,1)}), bf16[4,24,2048]{2,1,0:T(8,128)(2,1)S(1)}, u32[]{:S(2)}, u32[]{:S(2)}) async-start(bf16[4,24,2048]{2,1,0:T(8,128)(2,1)} %bitcast.12), calls=%async_computation.6 | async-start | bytes 786432 | tf_op jit(solution)/shard_map/all_to_all | solution.py:236
  156.6 12.1 %all-to-all-done.6.pieces_ref = bf16[4,24,2048]{2,1,0:T(8,128)(2,1)S(1)} async-done(((bf16[4,24,2048]{2,1,0:T(8,128)(2,1)}), bf16[4,24,2048]{2,1,0:T(8,128)(2,1)S(1)}, u32[]{:S(2)}, u32[]{:S(2)}) %all-to-all-start.6) | async-done | bytes 393248 | tf_op jit(solution)/shard_map/all_to_all | solution.py:236
  168.6 0.9 shard_map.78
  169.6 3.4 %all-to-all-start.7 = ((bf16[8,24,256]{2,1,0:T(8,128)(2,1)}), bf16[8,24,256]{2,1,0:T(8,128)(2,1)S(1)}, u32[]{:S(2)}, u32[]{:S(2)}) async-start(bf16[8,24,256]{2,1,0:T(8,128)(2,1)} %get-tuple-element.12), calls=%async_computation.7 | async-start | bytes 196608 | tf_op jit(solution)/shard_map/all_to_all | solution.py:242
  173.3 6.1 %all-to-all-done.7.tiles_ref = bf16[8,24,256]{2,1,0:T(8,128)(2,1)S(1)} async-done(((bf16[8,24,256]{2,1,0:T(8,128)(2,1)}), bf16[8,24,256]{2,1,0:T(8,128)(2,1)S(1)}, u32[]{:S(2)}, u32[]{:S(2)}) %all-to-all-start.7) | async-done | bytes 98336 | tf_op jit(solution)/shard_map/all_to_all | solution.py:242
  179.4 0.8 shard_map.79
  (45 shorter events, 2.1 us)
Async XLA Ops:
  0.0 14.4 %copy-start.2 = (s32[16,4]{0,1:T(4,128)S(1)}, s32[16,4]{0,1:T(4,128)}, u32[]{:S(2)}) copy-start(s32[16,4]{0,1:T(4,128)} %param.10) | copy-start | bytes 772
  2.9 23.2 %all-to-all-start = ((bf16[16,24,384]{2,1,0:T(8,128)(2,1)}), bf16[16,24,384]{2,1,0:T(8,128)(2,1)S(1)}, u32[]{:S(2)}, u32[]{:S(2)}) async-start(bf16[16,24,384]{2,1,0:T(8,128)(2,1)} %pad_maximum_fusion), calls=%async_computation | async-start | bytes 589824 | tf_op jit(solution)/shard_map/all_to_all | solution.py:174
  17.0 15.6 %collective-permute-start = (bf16[2048,512]{1,0:T(8,128)(2,1)S(1)}, bf16[2048,512]{1,0:T(8,128)(2,1)}, u32[]{:S(2)}, u32[]{:S(2)}) collective-permute-start(bf16[2048,512]{1,0:T(8,128)(2,1)S(1)} %bitcast_multiply_fusion.own_ref), channel_id=1, source_target_pairs={{0,1},{1,0},{2,3},{3,2},{4,5},{5,4},{6,7},{7,6},{8,9},{9,8},{10,11... | collective-permute-start | bytes 6291464 | tf_op jit(solution)/shard_map/ppermute | solution.py:168
  27.7 16.4 %all-to-all-start.1 = ((bf16[8,384,128]{2,1,0:T(8,128)(2,1)}), bf16[8,384,128]{2,1,0:T(8,128)(2,1)S(1)}, u32[]{:S(2)}, u32[]{:S(2)}) async-start(bf16[8,384,128]{2,1,0:T(8,128)(2,1)} %broadcast_in_dim.63), calls=%async_computation.1 | async-start | bytes 1572864 | tf_op jit(solution)/shard_map/all_to_all | solution.py:213
  49.3 6.3 %copy-start.1 = (s32[768]{0:T(1024)S(1)}, s32[768]{0:T(1024)}, u32[]{:S(2)}) copy-start(s32[768]{0:T(1024)} %param.11) | copy-start | bytes 9220
  49.3 6.7 %copy-start.4 = (f32[32]{0:T(128)S(1)}, f32[32]{0:T(128)}, u32[]{:S(2)}) copy-start(f32[32]{0:T(128)} %param.12) | copy-start | bytes 388
  49.3 6.8 %copy-start.3 = (f32[128]{0:T(128)S(1)}, f32[128]{0:T(128)}, u32[]{:S(2)}) copy-start(f32[128]{0:T(128)} %param.13) | copy-start | bytes 1540
  49.3 23.4 %all-to-all-start.2 = ((bf16[4,4,384,128]{3,2,1,0:T(8,128)(2,1)}), bf16[4,4,384,128]{3,2,1,0:T(8,128)(2,1)S(1)}, u32[]{:S(2)}, u32[]{:S(2)}) async-start(bf16[4,4,384,128]{3,2,1,0:T(8,128)(2,1)} %shard_map.74), calls=%async_computation.2 | async-start | bytes 3145728 | tf_op jit(solution)/shard_map/all_to_all | solution.py:215
  73.7 13.7 %all-to-all-start.3 = ((bf16[4,384,128]{2,1,0:T(8,128)(2,1)}), bf16[4,384,128]{2,1,0:T(8,128)(2,1)S(1)}, u32[]{:S(2)}, u32[]{:S(2)}) async-start(bf16[4,384,128]{2,1,0:T(8,128)(2,1)} %reduce_sum.60), calls=%async_computation.3 | async-start | bytes 786432 | tf_op jit(solution)/shard_map/all_to_all | solution.py:217
  87.5 2.2 %collective-permute-start.1 = (bf16[384,128]{1,0:T(8,128)(2,1)S(1)}, bf16[384,128]{1,0:T(8,128)(2,1)S(1)}, u32[]{:S(2)}, u32[]{:S(2)}) collective-permute-start(bf16[384,128]{1,0:T(8,128)(2,1)S(1)} %get-tuple-element.10), channel_id=1, source_target_pairs={{0,0},{1,1},{2,2},{3,3},{4,32},{5,33},{6,34},{7,35},{8,64},{9,65},... | collective-permute-start | bytes 294920 | tf_op jit(solution)/shard_map/ppermute | solution.py:223
  88.1 15.5 %collective-permute-start.2 = (bf16[384,128]{1,0:T(8,128)(2,1)S(1)}, bf16[384,128]{1,0:T(8,128)(2,1)S(1)}, u32[]{:S(2)}, u32[]{:S(2)}) collective-permute-start(bf16[384,128]{1,0:T(8,128)(2,1)S(1)} %get-tuple-element.10), channel_id=1, source_target_pairs={{0,2},{1,3},{2,0},{3,1},{4,34},{5,35},{6,32},{7,33},{8,66},{9,67},... | collective-permute-start | bytes 294920 | tf_op jit(solution)/shard_map/ppermute | solution.py:224
  147.7 31.7 %copy-start = (f32[24,2048]{1,0:T(8,128)S(1)}, f32[24,2048]{1,0:T(8,128)}, u32[]{:S(2)}) copy-start(f32[24,2048]{1,0:T(8,128)} %driver_ref.1) | copy-start | bytes 589828
  148.8 19.8 %all-to-all-start.6 = ((bf16[4,24,2048]{2,1,0:T(8,128)(2,1)}), bf16[4,24,2048]{2,1,0:T(8,128)(2,1)S(1)}, u32[]{:S(2)}, u32[]{:S(2)}) async-start(bf16[4,24,2048]{2,1,0:T(8,128)(2,1)} %bitcast.12), calls=%async_computation.6 | async-start | bytes 786432 | tf_op jit(solution)/shard_map/all_to_all | solution.py:236
  169.6 9.8 %all-to-all-start.7 = ((bf16[8,24,256]{2,1,0:T(8,128)(2,1)}), bf16[8,24,256]{2,1,0:T(8,128)(2,1)S(1)}, u32[]{:S(2)}, u32[]{:S(2)}) async-start(bf16[8,24,256]{2,1,0:T(8,128)(2,1)} %get-tuple-element.12), calls=%async_computation.7 | async-start | bytes 196608 | tf_op jit(solution)/shard_map/all_to_all | solution.py:242

commit v2 on v1

v2 whole, which is shorter than its diff:
```python
import jax
import jax.numpy as jnp
from jax import lax
from jax.experimental import pallas as pl
from jax.experimental.pallas import tpu as pltpu
from jax.sharding import Mesh, PartitionSpec as P

NV = 128
NOCC = 32
BLK = 128
SIDE = 16
BF = jnp.bfloat16
F32 = jnp.float32
AB = ("y", "zl")
GRID = ("x", "zh")
ALL = ("y", "zl", "zh", "x", "core")
VMEM = pl.BlockSpec(memory_space=pltpu.VMEM)
ANY = pl.BlockSpec(memory_space=pl.ANY)
SMEM = pl.BlockSpec(memory_space=pltpu.SMEM)
MIB = 1 << 20
SMALL = 12 * MIB
LARGE = 58 * MIB


def shape(*dims, dtype=BF):
    return jax.ShapeDtypeStruct(dims, dtype)


def call(kernel, out_shape, inputs, scalars=0, limit=SMALL):
    specs = [SMEM] * scalars + [VMEM] * (len(inputs) - scalars)
    outs = jax.tree.map(lambda _: VMEM, out_shape)
    return pl.pallas_call(
        kernel,
        out_shape=out_shape,
        in_specs=specs,
        out_specs=outs,
        compiler_params=pltpu.CompilerParams(vmem_limit_bytes=limit),
    )(*inputs)


def ones_where(condition):
    return condition.astype(F32).astype(BF)


def iotas(rows, cols):
    return (
        lax.broadcasted_iota(jnp.int32, (rows, cols), 0),
        lax.broadcasted_iota(jnp.int32, (rows, cols), 1),
    )


def turned(index):
    return index % SIDE * SIDE + index // SIDE


def pack_kernel(amplitudes_hbm, driver_hbm, out_ref, amplitudes_ref, driver_ref, sems):
    n_x, n_zh, _, width = out_ref.shape
    width = width // 2
    step = n_x * width
    copies = []
    for i in range(n_zh):
        here = slice(i * step, (i + 1) * step)
        copies.append(pltpu.make_async_copy(amplitudes_hbm.at[:, here], amplitudes_ref.at[:, here], sems.at[0, i]))
        copies.append(pltpu.make_async_copy(driver_hbm.at[:, here], driver_ref.at[:, here], sems.at[1, i]))
    for copy in copies:
        copy.start()
    for i in range(n_zh):
        copies[2 * i].wait()
        copies[2 * i + 1].wait()
        for x in range(n_x):
            here = slice((i * n_x + x) * width, (i * n_x + x + 1) * width)
            out_ref[x, i, :, :width] = amplitudes_ref[:, here].astype(BF)
            out_ref[x, i, :, width:] = driver_ref[:, here].astype(BF)


def pack_columns(amplitudes, driver, n_x, n_zh):
    rows, cols = amplitudes.shape
    return pl.pallas_call(
        pack_kernel,
        out_shape=shape(n_x, n_zh, rows, 2 * cols // (n_x * n_zh)),
        in_specs=[ANY, ANY],
        out_specs=VMEM,
        scratch_shapes=[pltpu.VMEM((rows, cols), F32)] * 2 + [pltpu.SemaphoreType.DMA((2, n_zh))],
        compiler_params=pltpu.CompilerParams(vmem_limit_bytes=SMALL),
    )(amplitudes, driver)


def mask_kernel(mask_ref, other_mask_ref, ladder_ref, other_ref, out_ref, other_out_ref):
    step = pl.program_id(0) * (ladder_ref.shape[0] // BLK)
    for mask, source, out in ((mask_ref, ladder_ref, out_ref), (other_mask_ref, other_ref, other_out_ref)):
        for i in range(source.shape[0] // BLK):
            rows = slice(i * BLK, (i + 1) * BLK)
            for t in range(source.shape[1] // BLK):
                cols = slice(t * BLK, (t + 1) * BLK)
                block = source[rows, cols]
                out[rows, cols] = jnp.where(mask[t, step + i] != 0, block, jnp.zeros_like(block))


def mask_ladder(block_mask, other_mask, ladder, other):
    rows, cols = ladder.shape
    block = pl.BlockSpec((rows // 4, cols), lambda n: (n, 0))
    return pl.pallas_call(
        mask_kernel,
        grid=(4,),
        out_shape=(shape(rows, cols), shape(rows, cols)),
        in_specs=[SMEM, SMEM, block, block],
        out_specs=(block, block),
        compiler_params=pltpu.CompilerParams(vmem_limit_bytes=LARGE),
        cost_estimate=pl.CostEstimate(flops=1 << 20, bytes_accessed=8 * MIB, transcendentals=0),
    )(block_mask, other_mask, ladder, other)


def send_kernel(mine_ref, masked_ref, turn_ref, *send_refs):
    mine = mine_ref[0]
    area = SIDE * SIDE
    half = area // 2
    count = masked_ref.shape[0] // area
    row, col = iotas(half, area)
    full_row, full_col = iotas(area, area)
    for j in range(count):
        b = lax.rem(mine + j, count)
        tile = masked_ref[pl.ds(pl.multiple_of(b * area, area), area), :]
        if j == 0:
            turn = ones_where(full_col == turned(full_row))
            turn_ref[...] = jnp.dot(turn, tile, preferred_element_type=F32).astype(BF)
        else:
            sent = ones_where(col == jnp.where(mine < b, half + row, turned(row)))
            send_refs[j - 1][...] = jnp.dot(sent, tile, preferred_element_type=F32).astype(BF)


def join_kernel(*refs):
    out_ref = refs[-1]
    at = 0
    for ref in refs[:-1]:
        out_ref[at : at + ref.shape[0], :] = ref[...]
        at += ref.shape[0]


def keep_kernel(mine_ref, own_ref, other_ref, keep_ref):
    mine = mine_ref[0]
    area = SIDE * SIDE
    half = area // 2
    count = own_ref.shape[0] // area
    depth = own_ref.shape[1]
    row, col = iotas(half, area)
    for j in range(count):
        b = lax.rem(mine + j, count)
        kept = ones_where(col == jnp.where(mine < b, row, turned(half + row)))
        for i, ref in enumerate((own_ref, other_ref)):
            cols = slice(i * depth, (i + 1) * depth)
            tile = ref[pl.ds(pl.multiple_of(b * area, area), area), :]
            if j == 0:
                keep_ref[(count - 1) * half :, cols] = tile
            else:
                keep_ref[(j - 1) * half : j * half, cols] = jnp.dot(
                    kept, tile, preferred_element_type=F32
                ).astype(BF)


def times(left, right):
    return lax.dot_general(left, right, (((1,), (1,)), ((), ())), preferred_element_type=F32)


def store_halves(core_ref, low_ref, out_ref):
    first = core_ref[0] == 0
    half = BLK // 2
    count = low_ref.shape[0]
    for s in range(0, count, 2):
        a, b = low_ref[s], low_ref[s + 1]
        zero = jnp.concatenate([a[:, :half], b[:, :half]], axis=1)
        one = jnp.concatenate([a[:, half:], b[:, half:]], axis=1)
        out_ref[:, s // 2 * BLK : (s // 2 + 1) * BLK] = jnp.where(first, zero, one)
        at = (count + s) // 2 * BLK
        out_ref[:, at : at + BLK] = jnp.where(first, one, zero)


def columns_kernel(core_ref, low_ref, own_ref, other_ref, out_ref, held_ref):
    depth = own_ref.shape[1]

    @pl.when(pl.program_id(0) == 0)
    def _():
        store_halves(core_ref, low_ref, held_ref)

    step = 256
    for n in range(own_ref.shape[0] // step):
        here = slice(n * step, (n + 1) * step)
        part = times(held_ref[:, :depth], own_ref[here, :]) + times(held_ref[:, depth:], other_ref[here, :])
        part = part.astype(BF)
        for j in range(step // BLK):
            out_ref[n * (step // BLK) + j, 0] = part[:, j * BLK : (j + 1) * BLK]


def columns_product(which_core, low, own, other, n_x, n_zh):
    n_ab, many, wide = low.shape
    out_rows, depth = own.shape
    block = pl.BlockSpec((out_rows // n_zh, depth), lambda n: (n, 0))
    return pl.pallas_call(
        columns_kernel,
        grid=(n_zh,),
        out_shape=shape(n_x, n_zh, many, wide),
        in_specs=[SMEM, pl.BlockSpec((n_ab, many, wide), lambda n: (0, 0, 0)), block, block],
        out_specs=pl.BlockSpec((n_x, 1, many, wide), lambda n: (0, n, 0, 0)),
        scratch_shapes=[pltpu.VMEM((many, 2 * depth), BF)],
        compiler_params=pltpu.CompilerParams(vmem_limit_bytes=LARGE),
        cost_estimate=pl.CostEstimate(flops=2 << 30, bytes_accessed=7 * MIB, transcendentals=0),
    )(which_core, low, own, other)


def rows_kernel(core_ref, low_ref, diag_ref, keep_ref, mown_ref, mother_ref, out_ref, held_ref, swap_ref):
    n_x, rows, _ = out_ref.shape
    depth = mown_ref.shape[1]

    @pl.when(pl.program_id(0) == 0)
    def _():
        store_halves(core_ref, low_ref, held_ref)
        row, col = iotas(BLK, BLK)
        other = row + 1 - 2 * (row % 2)
        for i in range(held_ref.shape[0] // BLK):
            here = slice(i * BLK, (i + 1) * BLK)
            swap = ones_where(col == jnp.where(diag_ref[here, :] != 0, row, other))
            swap_ref[here, :] = jnp.dot(swap, held_ref[here, :], preferred_element_type=F32).astype(BF)

    part = times(held_ref[...], keep_ref[...])
    part = part + times(swap_ref[:, :depth], mown_ref[...]) + times(swap_ref[:, depth:], mother_ref[...])
    part = part.astype(BF)
    for k in range(n_x):
        out_ref[k] = part[k * rows : (k + 1) * rows]


def rows_product(which_core, low, diag, keep, mown, mother, n_x):
    n_ab, many, wide = low.shape
    width, depth = mown.shape
    step = 384
    block = pl.BlockSpec((step, depth), lambda n: (n, 0))
    return pl.pallas_call(
        rows_kernel,
        grid=(width // step,),
        out_shape=shape(n_x, many // n_x, width),
        in_specs=[
            SMEM,
            pl.BlockSpec((n_ab, many, wide), lambda n: (0, 0, 0)),
            pl.BlockSpec((many, 1), lambda n: (0, 0)),
            pl.BlockSpec((step, 2 * depth), lambda n: (n, 0)),
            block,
            block,
        ],
        out_specs=pl.BlockSpec((n_x, many // n_x, step), lambda n: (0, 0, n)),
        scratch_shapes=[pltpu.VMEM((many, 2 * depth), BF)] * 2,
        compiler_params=pltpu.CompilerParams(vmem_limit_bytes=LARGE),
        cost_estimate=pl.CostEstimate(flops=2 << 30, bytes_accessed=7 * MIB, transcendentals=0),
    )(which_core, low, diag, keep, mown, mother)


def sum_leading(ref):
    total = ref[0].astype(F32)
    for i in range(1, ref.shape[0]):
        total = total + ref[i].astype(F32)
    return total


def swap_rows(values, diagonal):
    rows = values.shape[0]
    up = pltpu.roll(values, rows - 1, 0)
    down = pltpu.roll(values, 1, 0)
    even = lax.broadcasted_iota(jnp.int32, values.shape, 0) % 2 == 0
    return jnp.where(diagonal != 0, values, jnp.where(even, up, down))


def open_columns_kernel(half_ref, pieces_ref, total_ref, same_ref, cross_ref):
    half = half_ref[0]
    total = sum_leading(pieces_ref)
    total_ref[...] = total
    low = total.astype(BF)
    middle = low.shape[0] // 2
    lane, out = iotas(BLK, BLK)
    for ref, which in ((same_ref, half), (cross_ref, 1 - half)):
        y = lane % SIDE
        place = y % 8 * 8 + lane // SIDE
        goes = y // 8 == which
        left = ones_where(goes & (out == place))
        right = ones_where(goes & (out == place + BLK // 2))
        packed = jnp.dot(low[:middle], left, preferred_element_type=F32)
        packed = packed + jnp.dot(low[middle:], right, preferred_element_type=F32)
        ref[...] = packed.astype(BF)


def close_columns_kernel(half_ref, total_ref, same_ref, cross_ref, driver_ref, den_ref, diag_ref, out_ref):
    half = half_ref[0]
    middle = same_ref.shape[0]
    lane, out = iotas(BLK, BLK)
    for part in range(2):
        rows = slice(part * middle, (part + 1) * middle)
        mirrored = 0.0
        for ref, which in ((same_ref, half), (cross_ref, 1 - half)):
            at = lane - part * (BLK // 2)
            inside = (at >= 0) & (at < BLK // 2)
            place = at // 8 * SIDE + which * 8 + at % 8
            spread = ones_where(inside & (out == place))
            mirrored = mirrored + jnp.dot(ref[...], spread, preferred_element_type=F32)
        mirrored = swap_rows(mirrored, diag_ref[rows, :])
        driver = driver_ref[rows, :].astype(F32)
        low = ((driver + (total_ref[rows, :] + mirrored)) / den_ref[rows, :]).astype(BF)
        for i in range(out_ref.shape[0]):
            out_ref[i, rows, :] = low


def open_rows_kernel(mine_ref, pieces_ref, total_ref, out_ref):
    mine = mine_ref[0]
    count, rows, half = out_ref.shape
    total = sum_leading(pieces_ref)
    total_ref[...] = total
    out_ref[mine] = jnp.zeros((rows, half), BF)
    for j in range(1, count):
        out_ref[lax.rem(mine + j, count)] = total[:, (j - 1) * half : j * half].astype(BF)


def close_rows_kernel(mine_ref, total_ref, tiles_ref, driver_ref, row_ref, col_ref, diag_ref, out_ref):
    mine = mine_ref[0]
    count, _, half = tiles_ref.shape
    area = 2 * half
    lane, out = iotas(area, area)
    turn = (lane == turned(out)).astype(F32)
    for j in range(count):
        b = lax.rem(mine + j, count)
        if j == 0:
            symmetric = total_ref[:, (count - 1) * half :]
        else:
            own = total_ref[:, (j - 1) * half : j * half]
            theirs = swap_rows(tiles_ref[b].astype(F32), diag_ref[...])
            behind = jnp.dot(
                jnp.concatenate([theirs, own], axis=1),
                turn,
                precision=lax.Precision.HIGHEST,
                preferred_element_type=F32,
            )
            symmetric = jnp.where(mine < b, jnp.concatenate([own, theirs], axis=1), behind)
        here = pl.ds(pl.multiple_of(b * area, area), area)
        den = col_ref[:, here] - row_ref[...]
        out_ref[:, here] = (driver_ref[:, here] + symmetric) / den


def pick(table, index):
    hit = index[:, None] == jnp.arange(table.shape[0], dtype=jnp.int32)[None, :]
    return jnp.sum(jnp.where(hit, table[None, :], jnp.zeros((), table.dtype)), axis=1)


def body(amplitudes, driver, ladder, block_mask, pair_list, occ_energy, virt_energy):
    n_x, n_zh, n_core = lax.axis_size("x"), lax.axis_size("zh"), lax.axis_size("core")
    n_ab = lax.axis_size(AB)
    cells = n_x * n_zh
    core, ix, izh = lax.axis_index("core"), lax.axis_index("x"), lax.axis_index("zh")
    ab_index = lax.axis_index(AB)
    mine = ab_index.astype(jnp.int32).reshape(1)
    which_core = core.astype(jnp.int32).reshape(1)
    rows, cols = amplitudes.shape
    out_rows, in_cols = ladder.shape
    wide = cols // cells
    many = rows * cells
    area = SIDE * SIDE
    kept = (n_ab - 1) * (area // 2) + area
    swap_core = [(0, 1), (1, 0)]

    pack = pack_columns(amplitudes, driver, n_x, n_zh)
    pack = lax.all_to_all(pack.reshape(cells, rows, 2 * wide), GRID, 0, 0, tiled=True).reshape(many, 2 * wide)
    start = pack[:, :wide]
    drv = pack[:, wide:]

    other = lax.ppermute(ladder, "core", swap_core)
    other_mask = lax.ppermute(block_mask.T, "core", swap_core)
    _, other, other_mask, ladder = lax.optimization_barrier((pack, other, other_mask, ladder))
    own, other = mask_ladder(block_mask.T, other_mask, ladder, other)

    m = jnp.arange(many, dtype=jnp.int32)
    at = m // rows % n_zh * n_x + m // rows // n_zh
    local = pick(pair_list, (at * n_core + core) * rows + m % rows)
    row_energy = pick(occ_energy, local // NOCC) + pick(occ_energy, local % NOCC)
    diag = (local // NOCC == local % NOCC).astype(jnp.int32)
    pairs = ab_index * cols + jnp.arange(cols, dtype=jnp.int32)
    first = pairs // (SIDE * NV) * SIDE + pairs // SIDE % SIDE
    second = pairs // area % n_ab * SIDE + pairs % SIDE
    col_energy = pick(virt_energy, first) + pick(virt_energy, second)
    cell = izh * n_x + ix
    here = lax.dynamic_slice_in_dim(col_energy, cell * wide, wide)
    den = here[None, :] - row_energy[:, None]
    at = (ix * n_zh + izh) * rows
    my_rows = lax.dynamic_slice_in_dim(row_energy, at, rows)
    my_diag = lax.dynamic_slice_in_dim(diag, at, rows)
    half = (cell % 2).astype(jnp.int32).reshape(1)

    def place(a, q, c):
        return ((a * (n_zh * n_x)) + q) * n_core + c

    same, cross = [], []
    for a in range(n_ab):
        for q in range(cells):
            for c in range(n_core):
                b, h = q // 2, q % 2
                same.append((place(a, q, c), place(b, 2 * a + h, c)))
                cross.append((place(a, q, c), place(b, 2 * a + 1 - h, c)))

    low = lax.all_to_all(jnp.broadcast_to(start[None], (n_ab, many, wide)), AB, 0, 0, tiled=True)
    part = columns_product(which_core, low, own, other, n_x, n_zh)
    part, later = lax.optimization_barrier((part, own))
    part = lax.all_to_all(part, "x", 0, 0, tiled=True)

    turn, *send = call(
        send_kernel,
        (shape(area, in_cols),) + (shape(area // 2, in_cols),) * (n_ab - 1),
        [mine, later],
        1,
    )
    slots = [None] * n_ab

    def pass_on(j, block):
        slots[n_ab - j] = lax.ppermute(block, AB, [(k, (k + j) % n_ab) for k in range(n_ab)])

    for j in range(1, n_ab, 2):
        pass_on(j, send[j - 1])
    part, slots[1::2], send = lax.optimization_barrier((part, slots[1::2], send))

    part = jnp.sum(part.astype(F32), axis=0).astype(BF)
    part = lax.all_to_all(part, "zh", 0, 0, tiled=True)
    for j in range(2, n_ab, 2):
        pass_on(j, send[j - 1])
    part, slots[2::2] = lax.optimization_barrier((part, slots[2::2]))
    mirror = call(join_kernel, shape(kept, in_cols), slots[1:] + [turn])
    mirror_other = lax.ppermute(mirror, "core", swap_core)

    total, to_same, to_cross = call(
        open_columns_kernel,
        (shape(many, wide, dtype=F32), shape(many // 2, wide), shape(many // 2, wide)),
        [half, part],
        1,
    )
    from_same = lax.ppermute(to_same, ALL, same)
    from_cross = lax.ppermute(to_cross, ALL, cross)
    low = call(
        close_columns_kernel,
        shape(n_ab, many, wide),
        [half, total, from_same, from_cross, drv, den, diag[:, None]],
        1,
    )

    low, later, later_other = lax.optimization_barrier((low, own, other))
    low = lax.all_to_all(low, AB, 0, 0, tiled=True)
    keep = call(keep_kernel, shape(kept, 2 * in_cols), [mine, later, later_other], 1, LARGE)
    part = rows_product(which_core, low, diag[:, None], keep, mirror, mirror_other, n_x)
    part = lax.all_to_all(part, "x", 0, 0, tiled=True)
    part = jnp.sum(part.astype(F32), axis=0).astype(BF).reshape(n_zh, rows, kept)
    part = lax.all_to_all(part, "zh", 0, 0, tiled=True)
    total, tiles = call(
        open_rows_kernel,
        (shape(rows, kept, dtype=F32), shape(n_ab, rows, area // 2)),
        [mine, part],
        1,
    )
    tiles = lax.all_to_all(tiles, AB, 0, 0, tiled=True)
    return call(
        close_rows_kernel,
        shape(rows, cols, dtype=F32),
        [mine, total, tiles, driver, my_rows[:, None], col_energy[None, :], my_diag[:, None]],
        1,
    )


def solution(mesh):
    fine = Mesh(mesh.devices.reshape(4, 2, 4, 4, 2), ALL)
    ab, cd = AB, ("zh", "x", "core")
    placed = (P(cd, ab), P(cd, ab), P(ab, cd), P(ab, cd), P(), P(), P())
    return jax.shard_map(body, mesh=fine, in_specs=placed, out_specs=P(cd, ab), check_vma=False)
```

time: 181 us -> 176 us (0.972)
  waiting for transfers between devices: 72.2 us -> 46.6 us
  starting transfers between devices: 39.5 us -> 52.9 us
  Pallas kernels: 16.7 us -> 26.4 us
  blocking collectives: 39.8 us -> 36 us
  local copies, waits for them, and re-layouts: 3.24 us -> 7.02 us
  other arithmetic: 8.49 us -> 5.5 us
    pallas_call x0 -> x4, Pallas kernels: none -> 17.7 us  [the longest x1 6.62 us: rows_product(): pl.pallas_call(rows_kernel, grid=(width // step,), out_shape=shape(n_x, m...]
    all_to_all x2, waiting for transfers between devices: 21.9 us -> 10.2 us  [body(): part = lax.all_to_all(part, 'zh', 0, 0, tiled=True)]
    all_to_all x1, waiting for transfers between devices: 15.2 us -> 4.1 us  [body(): part = lax.all_to_all(part, 'x', 0, 0, tiled=True)]
    ppermute x3 -> x12, starting transfers between devices: 2.31 us -> 12 us  [the longest x7 9.39 us: pass_on(): lax.ppermute(block, AB, [(k, (k + j) % n_ab) for k in range(n_ab)])]
    pallas_call x7, Pallas kernels: 16.7 us -> 8.65 us  [call(): pl.pallas_call(kernel, out_shape=out_shape, in_specs=specs, out_specs=out...]
    all_to_all x1, blocking collectives: 22.3 us -> 14.4 us  [body(): part = lax.all_to_all(part, 'x', 0, 0, tiled=True)]
    all_to_all x2, starting transfers between devices: 14.8 us -> 21.7 us  [the longest x1 16.4 us: body(): low = lax.all_to_all(low, AB, 0, 0, tiled=True)]
    unnamed x11 -> x30, local copies, waits for them, and re-layouts: 0.03 us -> 5.61 us
  transfers between devices with their start and end apart: 9 -> 18, of which waited for: 7 -> 14; matrix products, arithmetic and copies ran while one was open for 4% -> 2% of each run, Pallas kernels for 3% -> 6%
where the time goes in v2:
time: 176 us; the launch traced here: 175 us
  starting transfers between devices  52.9 us (30%)
  waiting for transfers between devices  46.6 us (26%)
  blocking collectives  36 us (20%)
  Pallas kernels  26.4 us (15%)
  local copies, waits for them, and re-layouts  7.02 us (4%)
  other arithmetic  5.5 us (3%)
    all_to_all x1, blocking collectives, body(): lax.all_to_all(pack.reshape(cells, rows, 2 * wide), GRID, 0, 0, tiled=True)  21.6 us
    all_to_all x1, starting transfers between devices, body(): low = lax.all_to_all(low, AB, 0, 0, tiled=True)  16.4 us
    all_to_all x1, blocking collectives, body(): part = lax.all_to_all(part, 'x', 0, 0, tiled=True)  14.4 us
    ppermute x7, waiting for transfers between devices, pass_on(): lax.ppermute(block, AB, [(k, (k + j) % n_ab) for k in range(n_ab)])  12.4 us
    all_to_all x2, waiting for transfers between devices, body(): part = lax.all_to_all(part, 'zh', 0, 0, tiled=True)  10.2 us
    ppermute x7, starting transfers between devices, pass_on(): lax.ppermute(block, AB, [(k, (k + j) % n_ab) for k in range(n_ab)])  9.39 us
    pallas_call x7, Pallas kernels, call(): pl.pallas_call(kernel, out_shape=out_shape, in_specs=specs, out_specs=out...  8.65 us
    all_to_all x1, starting transfers between devices, body(): part = lax.all_to_all(part, 'x', 0, 0, tiled=True)  7.16 us
  transfers between devices with their start and end apart: 18, of which 14 were waited for; matrix products, arithmetic and copies ran while one was open for 2% of the time, Pallas kernels for 6%

profile of v2, /device:TPU:2, one launch (start us, length us, event | category | flops | bytes accessed | tf_op | source)
XLA Modules:
  0.0 174.6 jit_solution(8724136865834488321)
XLA Ops:
  2.2 21.6 %all_to_all.40 = bf16[16,24,256]{2,1,0:T(8,128)(2,1)S(1)} all-to-all(bf16[16,24,256]{2,1,0:T(8,128)(2,1)S(1)} %bitcast.12), channel_id=1, replica_groups=mesh['y'=4,'zl'=2,'zh'=4,'x'=4,'core'=2] {'x','zh'}, dimensions={0} | all-to-all | bytes 393216 | tf_op jit(solution)/shard_map/all_to_all | solution.py:364
  24.7 4.9 %all-to-all-start.1 = ((bf16[8,384,128]{2,1,0:T(8,128)(2,1)}), bf16[8,384,128]{2,1,0:T(8,128)(2,1)S(1)}, u32[]{:S(2)}, u32[]{:S(2)}) async-start(bf16[8,384,128]{2,1,0:T(8,128)(2,1)} %broadcast_in_dim.76), calls=%async_computation.1 | async-start | bytes 1572864 | tf_op jit(solution)/shard_map/all_to_all | solution.py:401
  31.5 1.3 copy-done.6
  32.8 5.1 %shard_map.74 = (bf16[2048,512]{1,0:T(8,128)(2,1)}, bf16[2048,512]{1,0:T(8,128)(2,1)}) custom-call(s32[4,16]{1,0:T(4,128)} %bitcast.15, s32[4,16]{1,0:T(4,128)} %copy-done.11, bf16[2048,512]{1,0:T(8,128)(2,1)} %ladder_ref, bf16[2048,512]{1,0:T(8,128)(2,1)} %copy-done.6), custom_call_target="tpu_custom_call" | custom-call | flops 1048576 | bytes 8388608 | tf_op jit(solution)/shard_map/pallas_call | solution.py:102
  37.9 3.9 %all-to-all-done.1.low_ref = bf16[8,384,128]{2,1,0:T(8,128)(2,1)S(1)} async-done(((bf16[8,384,128]{2,1,0:T(8,128)(2,1)}), bf16[8,384,128]{2,1,0:T(8,128)(2,1)S(1)}, u32[]{:S(2)}, u32[]{:S(2)}) %all-to-all-start.1) | async-done | bytes 786464 | tf_op jit(solution)/shard_map/all_to_all | solution.py:401
  42.6 5.8 %shard_map.75 = bf16[4,4,384,128]{3,2,1,0:T(8,128)(2,1)} custom-call(s32[1]{0:T(128)} %bitcast.1.core_ref, bf16[8,384,128]{2,1,0:T(8,128)(2,1)} %copy-done.8, bf16[2048,512]{1,0:T(8,128)(2,1)} %get-tuple-element.63.own_ref.masked_ref, bf16[2048,512]{1,0:T(8,128)(2,1)} %get-tuple-element.64.other_ref), custom_call_target="tpu_custom_call" | custom-call | flops 2147483648 | bytes 7340032 | tf_op jit(solution)/shard_map/pallas_call | solution.py:197
  48.4 7.2 %all-to-all-start.2 = ((bf16[4,4,384,128]{3,2,1,0:T(8,128)(2,1)}), bf16[4,4,384,128]{3,2,1,0:T(8,128)(2,1)}, u32[]{:S(2)}, u32[]{:S(2)}) async-start(bf16[4,4,384,128]{3,2,1,0:T(8,128)(2,1)} %shard_map.75), calls=%async_computation.2 | async-start | bytes 3145728 | tf_op jit(solution)/shard_map/all_to_all | solution.py:404
  56.4 1.5 collective-permute-start.2
  58.9 2.0 %collective-permute-start.4 = (bf16[128,512]{1,0:T(8,128)(2,1)S(1)}, bf16[128,512]{1,0:T(8,128)(2,1)S(1)}, u32[]{:S(2)}, u32[]{:S(2)}) collective-permute-start(bf16[128,512]{1,0:T(8,128)(2,1)S(1)} %get-tuple-element.49), channel_id=1, source_target_pairs={{0,96},{32,128},{64,160},{96,192},{128,224},{160,0},{192,32},{224,... | collective-permute-start | bytes 393224 | tf_op jit(solution)/shard_map/ppermute | solution.py:415
  60.8 2.1 %collective-permute-start.5 = (bf16[128,512]{1,0:T(8,128)(2,1)S(1)}, bf16[128,512]{1,0:T(8,128)(2,1)S(1)}, u32[]{:S(2)}, u32[]{:S(2)}) collective-permute-start(bf16[128,512]{1,0:T(8,128)(2,1)S(1)} %get-tuple-element.50), channel_id=1, source_target_pairs={{0,32},{32,64},{64,96},{96,128},{128,160},{160,192},{192,224},{224... | collective-permute-start | bytes 393224 | tf_op jit(solution)/shard_map/ppermute | solution.py:415
  63.0 2.3 %collective-permute-done.3.refs_2_ = bf16[128,512]{1,0:T(8,128)(2,1)S(1)} collective-permute-done((bf16[128,512]{1,0:T(8,128)(2,1)S(1)}, bf16[128,512]{1,0:T(8,128)(2,1)S(1)}, u32[]{:S(2)}, u32[]{:S(2)}) %collective-permute-start.3) | collective-permute-done | bytes 131104 | tf_op jit(solution)/shard_map/ppermute | solution.py:415
  65.3 3.1 %collective-permute-done.4.refs_4_ = bf16[128,512]{1,0:T(8,128)(2,1)S(1)} collective-permute-done((bf16[128,512]{1,0:T(8,128)(2,1)S(1)}, bf16[128,512]{1,0:T(8,128)(2,1)S(1)}, u32[]{:S(2)}, u32[]{:S(2)}) %collective-permute-start.4) | collective-permute-done | bytes 131104 | tf_op jit(solution)/shard_map/ppermute | solution.py:415
  69.3 4.1 %all-to-all-done.2 = bf16[4,4,384,128]{3,2,1,0:T(8,128)(2,1)} async-done(((bf16[4,4,384,128]{3,2,1,0:T(8,128)(2,1)}), bf16[4,4,384,128]{3,2,1,0:T(8,128)(2,1)}, u32[]{:S(2)}, u32[]{:S(2)}) %all-to-all-start.2) | async-done | bytes 1572896 | tf_op jit(solution)/shard_map/all_to_all | solution.py:404
  73.4 2.5 %reduce_sum.71 = bf16[4,384,128]{2,1,0:T(8,128)(2,1)} reduce(bf16[4,4,384,128]{3,2,1,0:T(8,128)(2,1)} %all-to-all-done.2, bf16[]{:T(256)} %constant.156.clone.1), dimensions={0}, to_apply=%region_0.1 | reduce | flops 589824 | bytes 1966082 | tf_op jit(solution)/shard_map/reduce_sum | solution.py:421
  76.0 3.5 %all-to-all-start.3 = ((bf16[4,384,128]{2,1,0:T(8,128)(2,1)}), bf16[4,384,128]{2,1,0:T(8,128)(2,1)S(1)}, u32[]{:S(2)}, u32[]{:S(2)}) async-start(bf16[4,384,128]{2,1,0:T(8,128)(2,1)} %reduce_sum.71), calls=%async_computation.3 | async-start | bytes 786432 | tf_op jit(solution)/shard_map/all_to_all | solution.py:422
  79.6 1.3 select_reduce_fusion.1
  84.0 2.0 %collective-permute-done.6.refs_1_ = bf16[128,512]{1,0:T(8,128)(2,1)S(1)} collective-permute-done((bf16[128,512]{1,0:T(8,128)(2,1)S(1)}, bf16[128,512]{1,0:T(8,128)(2,1)S(1)}, u32[]{:S(2)}, u32[]{:S(2)}) %collective-permute-start.6) | collective-permute-done | bytes 131104 | tf_op jit(solution)/shard_map/ppermute | solution.py:415
  86.0 2.7 %collective-permute-done.7.refs_3_ = bf16[128,512]{1,0:T(8,128)(2,1)S(1)} collective-permute-done((bf16[128,512]{1,0:T(8,128)(2,1)S(1)}, bf16[128,512]{1,0:T(8,128)(2,1)S(1)}, u32[]{:S(2)}, u32[]{:S(2)}) %collective-permute-start.7) | collective-permute-done | bytes 131104 | tf_op jit(solution)/shard_map/ppermute | solution.py:415
  88.7 1.3 collective-permute-done.8.refs_5_
  92.0 1.5 collective-permute-start.10
  93.8 3.4 %collective-permute-done.10.cross_ref = bf16[192,128]{1,0:T(8,128)(2,1)S(1)} collective-permute-done((bf16[192,128]{1,0:T(8,128)(2,1)S(1)}, bf16[192,128]{1,0:T(8,128)(2,1)S(1)}, u32[]{:S(2)}, u32[]{:S(2)}) %collective-permute-start.10) | collective-permute-done | bytes 49184 | tf_op jit(solution)/shard_map/ppermute | solution.py:436
  97.2 1.2 shard_map.78
  98.5 16.4 %all-to-all-start.4 = ((bf16[8,384,128]{2,1,0:T(8,128)(2,1)}), bf16[8,384,128]{2,1,0:T(8,128)(2,1)S(1)}, u32[]{:S(2)}, u32[]{:S(2)}) async-start(bf16[8,384,128]{2,1,0:T(8,128)(2,1)} %shard_map.78), calls=%async_computation.4 | async-start | bytes 1572864 | tf_op jit(solution)/shard_map/all_to_all | solution.py:445
  115.3 4.4 %shard_map.79.keep_ref = bf16[1152,1024]{1,0:T(8,128)(2,1)} custom-call(s32[1]{0:T(128)} %bitcast.mine_ref, bf16[2048,512]{1,0:T(8,128)(2,1)} %get-tuple-element.63.own_ref.masked_ref, bf16[2048,512]{1,0:T(8,128)(2,1)} %get-tuple-element.64.other_ref), custom_call_target="tpu_custom_call" | custom-call | tf_op jit(solution)/shard_map/pallas_call | solution.py:32
  119.7 5.3 %all-to-all-done.4.low_ref = bf16[8,384,128]{2,1,0:T(8,128)(2,1)S(1)} async-done(((bf16[8,384,128]{2,1,0:T(8,128)(2,1)}), bf16[8,384,128]{2,1,0:T(8,128)(2,1)S(1)}, u32[]{:S(2)}, u32[]{:S(2)}) %all-to-all-start.4) | async-done | bytes 786464 | tf_op jit(solution)/shard_map/all_to_all | solution.py:445
  126.0 6.6 %shard_map.81 = bf16[4,96,1152]{2,1,0:T(8,128)(2,1)} custom-call(s32[1]{0:T(128)} %bitcast.1.core_ref, bf16[8,384,128]{2,1,0:T(8,128)(2,1)} %copy-done.7, s32[384,1]{1,0:T(8,128)} %copy-done.4, bf16[1152,1024]{1,0:T(8,128)(2,1)} %shard_map.79.keep_ref, bf16[1152,512]{1,0:T(8,128)(2,1)} %copy-done.1, bf16[1152,512]{1,0:T(8,128)(2,1)} %copy-done.14), custom_call_target="tpu_custom_call" | custom-call | flops 2147483648 | bytes 7340032 | tf_op jit(solution)/shard_map/pallas_call | solution.py:235
  132.6 14.4 %all_to_all.41 = bf16[4,96,1152]{2,1,0:T(8,128)(2,1)S(1)} all-to-all(bf16[4,96,1152]{2,1,0:T(8,128)(2,1)} %shard_map.81), channel_id=1, replica_groups=mesh['y'=4,'zl'=2,'zh'=4,'x'=4,'core'=2] {'x'}, dimensions={0} | all-to-all | bytes 1769472 | tf_op jit(solution)/shard_map/all_to_all | solution.py:448
  147.9 3.7 %all-to-all-start.6 = ((bf16[4,24,1152]{2,1,0:T(8,128)(2,1)}), bf16[4,24,1152]{2,1,0:T(8,128)(2,1)S(1)}, u32[]{:S(2)}, u32[]{:S(2)}) async-start(bf16[4,24,1152]{2,1,0:T(8,128)(2,1)} %bitcast.6), calls=%async_computation.6 | async-start | bytes 442368 | tf_op jit(solution)/shard_map/all_to_all | solution.py:450
  151.7 9.1 %all-to-all-done.6.pieces_ref = bf16[4,24,1152]{2,1,0:T(8,128)(2,1)S(1)} async-done(((bf16[4,24,1152]{2,1,0:T(8,128)(2,1)}), bf16[4,24,1152]{2,1,0:T(8,128)(2,1)S(1)}, u32[]{:S(2)}, u32[]{:S(2)}) %all-to-all-start.6) | async-done | bytes 221216 | tf_op jit(solution)/shard_map/all_to_all | solution.py:450
  161.4 5.3 %all-to-all-start.7 = ((bf16[8,24,128]{2,1,0:T(8,128)(2,1)}), bf16[8,24,128]{2,1,0:T(8,128)(2,1)S(1)}, u32[]{:S(2)}, u32[]{:S(2)}) async-start(bf16[8,24,128]{2,1,0:T(8,128)(2,1)} %get-tuple-element.74), calls=%async_computation.7 | async-start | bytes 98304 | tf_op jit(solution)/shard_map/all_to_all | solution.py:457
  166.9 6.1 %all-to-all-done.7.tiles_ref = bf16[8,24,128]{2,1,0:T(8,128)(2,1)S(1)} async-done(((bf16[8,24,128]{2,1,0:T(8,128)(2,1)}), bf16[8,24,128]{2,1,0:T(8,128)(2,1)S(1)}, u32[]{:S(2)}, u32[]{:S(2)}) %all-to-all-start.7) | async-done | bytes 49184 | tf_op jit(solution)/shard_map/all_to_all | solution.py:457
  173.0 1.6 shard_map.83
  (67 shorter events, 17.2 us)
Async XLA Ops:
  0.0 30.9 %collective-permute-start = (bf16[2048,512]{1,0:T(8,128)(2,1)}, bf16[2048,512]{1,0:T(8,128)(2,1)S(1)}, u32[]{:S(2)}, u32[]{:S(2)}) collective-permute-start(bf16[2048,512]{1,0:T(8,128)(2,1)} %ladder_ref), channel_id=1, source_target_pairs={{0,1},{1,0},{2,3},{3,2},{4,5},{5,4},{6,7},{7,6},{8,9},{9,8},{10,11... | collective-permute-start | bytes 6291464 | tf_op jit(solution)/shard_map/ppermute | solution.py:368
  0.0 0.9 copy-start.2
  0.9 0.9 copy-start.5
  2.1 27.5 %copy-start.10 = (s32[16,4]{0,1:T(4,128)S(1)}, s32[16,4]{0,1:T(4,128)}, u32[]{:S(2)}) copy-start(s32[16,4]{0,1:T(4,128)} %param.10) | copy-start | bytes 772
  24.7 17.0 %all-to-all-start.1 = ((bf16[8,384,128]{2,1,0:T(8,128)(2,1)}), bf16[8,384,128]{2,1,0:T(8,128)(2,1)S(1)}, u32[]{:S(2)}, u32[]{:S(2)}) async-start(bf16[8,384,128]{2,1,0:T(8,128)(2,1)} %broadcast_in_dim.76), calls=%async_computation.1 | async-start | bytes 1572864 | tf_op jit(solution)/shard_map/all_to_all | solution.py:401
  29.7 1.2 collective-permute-start.1
  31.5 1.3 copy-start.6
  41.7 0.9 copy-start.8
  48.4 7.2 %copy-start.9 = (s32[768]{0:T(1024)S(1)}, s32[768]{0:T(1024)}, u32[]{:S(2)}) copy-start(s32[768]{0:T(1024)} %param.11) | copy-start | bytes 9220
  48.4 7.5 %copy-start = (bf16[2048,512]{1,0:T(8,128)(2,1)S(1)}, bf16[2048,512]{1,0:T(8,128)(2,1)}, u32[]{:S(2)}) copy-start(bf16[2048,512]{1,0:T(8,128)(2,1)} %get-tuple-element.63.own_ref.masked_ref) | copy-start | bytes 6291460
  48.4 25.0 %all-to-all-start.2 = ((bf16[4,4,384,128]{3,2,1,0:T(8,128)(2,1)}), bf16[4,4,384,128]{3,2,1,0:T(8,128)(2,1)}, u32[]{:S(2)}, u32[]{:S(2)}) async-start(bf16[4,4,384,128]{3,2,1,0:T(8,128)(2,1)} %shard_map.75), calls=%async_computation.2 | async-start | bytes 3145728 | tf_op jit(solution)/shard_map/all_to_all | solution.py:404
  56.4 23.0 %copy-start.13 = (f32[32]{0:T(128)S(1)}, f32[32]{0:T(128)}, u32[]{:S(2)}) copy-start(f32[32]{0:T(128)} %param.12) | copy-start | bytes 388
  56.4 23.2 %copy-start.12 = (f32[128]{0:T(128)S(1)}, f32[128]{0:T(128)}, u32[]{:S(2)}) copy-start(f32[128]{0:T(128)} %param.13) | copy-start | bytes 1540
  56.4 6.5 %collective-permute-start.2 = (bf16[128,512]{1,0:T(8,128)(2,1)S(1)}, bf16[128,512]{1,0:T(8,128)(2,1)S(1)}, u32[]{:S(2)}, u32[]{:S(2)}) collective-permute-start(bf16[128,512]{1,0:T(8,128)(2,1)S(1)} %get-tuple-element.47), channel_id=1, source_target_pairs={{0,224},{32,0},{64,32},{96,64},{128,96},{160,128},{192,160},{224,1... | collective-permute-start | bytes 393224 | tf_op jit(solution)/shard_map/ppermute | solution.py:415
  57.9 7.3 %collective-permute-start.3 = (bf16[128,512]{1,0:T(8,128)(2,1)S(1)}, bf16[128,512]{1,0:T(8,128)(2,1)S(1)}, u32[]{:S(2)}, u32[]{:S(2)}) collective-permute-start(bf16[128,512]{1,0:T(8,128)(2,1)S(1)} %get-tuple-element.48), channel_id=1, source_target_pairs={{0,160},{32,192},{64,224},{96,0},{128,32},{160,64},{192,96},{224,1... | collective-permute-start | bytes 393224 | tf_op jit(solution)/shard_map/ppermute | solution.py:415
  58.9 9.5 %collective-permute-start.4 = (bf16[128,512]{1,0:T(8,128)(2,1)S(1)}, bf16[128,512]{1,0:T(8,128)(2,1)S(1)}, u32[]{:S(2)}, u32[]{:S(2)}) collective-permute-start(bf16[128,512]{1,0:T(8,128)(2,1)S(1)} %get-tuple-element.49), channel_id=1, source_target_pairs={{0,96},{32,128},{64,160},{96,192},{128,224},{160,0},{192,32},{224,... | collective-permute-start | bytes 393224 | tf_op jit(solution)/shard_map/ppermute | solution.py:415
  60.8 8.5 %collective-permute-start.5 = (bf16[128,512]{1,0:T(8,128)(2,1)S(1)}, bf16[128,512]{1,0:T(8,128)(2,1)S(1)}, u32[]{:S(2)}, u32[]{:S(2)}) collective-permute-start(bf16[128,512]{1,0:T(8,128)(2,1)S(1)} %get-tuple-element.50), channel_id=1, source_target_pairs={{0,32},{32,64},{64,96},{96,128},{128,160},{160,192},{192,224},{224... | collective-permute-start | bytes 393224 | tf_op jit(solution)/shard_map/ppermute | solution.py:415
  76.0 15.1 %all-to-all-start.3 = ((bf16[4,384,128]{2,1,0:T(8,128)(2,1)}), bf16[4,384,128]{2,1,0:T(8,128)(2,1)S(1)}, u32[]{:S(2)}, u32[]{:S(2)}) async-start(bf16[4,384,128]{2,1,0:T(8,128)(2,1)} %reduce_sum.71), calls=%async_computation.3 | async-start | bytes 786432 | tf_op jit(solution)/shard_map/all_to_all | solution.py:422
  81.0 5.0 %collective-permute-start.6 = (bf16[128,512]{1,0:T(8,128)(2,1)S(1)}, bf16[128,512]{1,0:T(8,128)(2,1)S(1)}, u32[]{:S(2)}, u32[]{:S(2)}) collective-permute-start(bf16[128,512]{1,0:T(8,128)(2,1)S(1)} %get-tuple-element.55), channel_id=1, source_target_pairs={{0,192},{32,224},{64,0},{96,32},{128,64},{160,96},{192,128},{224,1... | collective-permute-start | bytes 393224 | tf_op jit(solution)/shard_map/ppermute | solution.py:415
  82.1 6.6 %collective-permute-start.7 = (bf16[128,512]{1,0:T(8,128)(2,1)S(1)}, bf16[128,512]{1,0:T(8,128)(2,1)S(1)}, u32[]{:S(2)}, u32[]{:S(2)}) collective-permute-start(bf16[128,512]{1,0:T(8,128)(2,1)S(1)} %get-tuple-element.56), channel_id=1, source_target_pairs={{0,128},{32,160},{64,192},{96,224},{128,0},{160,32},{192,64},{224,... | collective-permute-start | bytes 393224 | tf_op jit(solution)/shard_map/ppermute | solution.py:415
  83.0 7.0 %collective-permute-start.8 = (bf16[128,512]{1,0:T(8,128)(2,1)S(1)}, bf16[128,512]{1,0:T(8,128)(2,1)S(1)}, u32[]{:S(2)}, u32[]{:S(2)}) collective-permute-start(bf16[128,512]{1,0:T(8,128)(2,1)S(1)} %get-tuple-element.57), channel_id=1, source_target_pairs={{0,64},{32,96},{64,128},{96,160},{128,192},{160,224},{192,0},{224,... | collective-permute-start | bytes 393224 | tf_op jit(solution)/shard_map/ppermute | solution.py:415
  91.3 2.5 %collective-permute-start.9 = (bf16[192,128]{1,0:T(8,128)(2,1)S(1)}, bf16[192,128]{1,0:T(8,128)(2,1)S(1)}, u32[]{:S(2)}, u32[]{:S(2)}) collective-permute-start(bf16[192,128]{1,0:T(8,128)(2,1)S(1)} %get-tuple-element.60), channel_id=1, source_target_pairs={{0,0},{1,1},{2,2},{3,3},{4,32},{5,33},{6,34},{7,35},{8,64},{9,65},... | collective-permute-start | bytes 147464 | tf_op jit(solution)/shard_map/ppermute | solution.py:435
  92.0 5.2 %collective-permute-start.10 = (bf16[192,128]{1,0:T(8,128)(2,1)S(1)}, bf16[192,128]{1,0:T(8,128)(2,1)S(1)}, u32[]{:S(2)}, u32[]{:S(2)}) collective-permute-start(bf16[192,128]{1,0:T(8,128)(2,1)S(1)} %get-tuple-element.61), channel_id=1, source_target_pairs={{0,2},{1,3},{2,0},{3,1},{4,34},{5,35},{6,32},{7,33},{8,66},{9,67},... | collective-permute-start | bytes 147464 | tf_op jit(solution)/shard_map/ppermute | solution.py:436
  93.8 4.7 %copy-start.4 = (s32[384,1]{1,0:T(8,128)}, s32[384,1]{1,0:T(8,128)S(1)}, u32[]{:S(2)}) copy-start(s32[384,1]{1,0:T(8,128)S(1)} %fusion.8.diag_ref) | copy-start | bytes 4612
  98.5 26.6 %all-to-all-start.4 = ((bf16[8,384,128]{2,1,0:T(8,128)(2,1)}), bf16[8,384,128]{2,1,0:T(8,128)(2,1)S(1)}, u32[]{:S(2)}, u32[]{:S(2)}) async-start(bf16[8,384,128]{2,1,0:T(8,128)(2,1)} %shard_map.78), calls=%async_computation.4 | async-start | bytes 1572864 | tf_op jit(solution)/shard_map/all_to_all | solution.py:445
  115.0 4.7 %copy-start.1 = (bf16[1152,512]{1,0:T(8,128)(2,1)}, bf16[1152,512]{1,0:T(8,128)(2,1)S(1)}, u32[]{:S(2)}) copy-start(bf16[1152,512]{1,0:T(8,128)(2,1)S(1)} %shard_map.80.mown_ref) | copy-start | bytes 3538948
  115.0 4.7 %collective-permute-start.11 = (bf16[1152,512]{1,0:T(8,128)(2,1)S(1)}, bf16[1152,512]{1,0:T(8,128)(2,1)S(1)}, u32[]{:S(2)}, u32[]{:S(2)}) collective-permute-start(bf16[1152,512]{1,0:T(8,128)(2,1)S(1)} %shard_map.80.mown_ref), channel_id=1, source_target_pairs={{0,1},{1,0},{2,3},{3,2},{4,5},{5,4},{6,7},{7,6},{8,9},{9,8},{10,11... | collective-permute-start | bytes 3538952 | tf_op jit(solution)/shard_map/ppermute | solution.py:427
  119.7 5.3 %copy-start.14 = (bf16[1152,512]{1,0:T(8,128)(2,1)}, bf16[1152,512]{1,0:T(8,128)(2,1)S(1)}, u32[]{:S(2)}) copy-start(bf16[1152,512]{1,0:T(8,128)(2,1)S(1)} %collective-permute-done.11.mother_ref) | copy-start | bytes 3538948
  125.0 0.9 copy-start.7
  132.6 40.4 %copy-start.3 = (f32[24,2048]{1,0:T(8,128)S(1)}, f32[24,2048]{1,0:T(8,128)}, u32[]{:S(2)}) copy-start(f32[24,2048]{1,0:T(8,128)} %driver_ref.1) | copy-start | bytes 589828
  147.9 12.9 %all-to-all-start.6 = ((bf16[4,24,1152]{2,1,0:T(8,128)(2,1)}), bf16[4,24,1152]{2,1,0:T(8,128)(2,1)S(1)}, u32[]{:S(2)}, u32[]{:S(2)}) async-start(bf16[4,24,1152]{2,1,0:T(8,128)(2,1)} %bitcast.6), calls=%async_computation.6 | async-start | bytes 442368 | tf_op jit(solution)/shard_map/all_to_all | solution.py:450
  161.4 11.6 %all-to-all-start.7 = ((bf16[8,24,128]{2,1,0:T(8,128)(2,1)}), bf16[8,24,128]{2,1,0:T(8,128)(2,1)S(1)}, u32[]{:S(2)}, u32[]{:S(2)}) async-start(bf16[8,24,128]{2,1,0:T(8,128)(2,1)} %get-tuple-element.74), calls=%async_computation.7 | async-start | bytes 98304 | tf_op jit(solution)/shard_map/all_to_all | solution.py:457
  (1 other events, 0.6 us)

commit v3 on v2

--- a/solution.py
+++ b/solution.py
@@ -19,7 +19,8 @@
 SMEM = pl.BlockSpec(memory_space=pltpu.SMEM)
 MIB = 1 << 20
 SMALL = 12 * MIB
-LARGE = 58 * MIB
+LARGE = 52 * MIB
+WHOLE = 60 * MIB
 
 
 def shape(*dims, dtype=BF):
@@ -81,7 +82,7 @@
         in_specs=[ANY, ANY],
         out_specs=VMEM,
         scratch_shapes=[pltpu.VMEM((rows, cols), F32)] * 2 + [pltpu.SemaphoreType.DMA((2, n_zh))],
-        compiler_params=pltpu.CompilerParams(vmem_limit_bytes=SMALL),
+        compiler_params=pltpu.CompilerParams(vmem_limit_bytes=WHOLE),
     )(amplitudes, driver)
 
 
@@ -181,25 +182,24 @@
     def _():
         store_halves(core_ref, low_ref, held_ref)
 
-    step = 256
-    for n in range(own_ref.shape[0] // step):
-        here = slice(n * step, (n + 1) * step)
-        part = times(held_ref[:, :depth], own_ref[here, :]) + times(held_ref[:, depth:], other_ref[here, :])
-        part = part.astype(BF)
-        for j in range(step // BLK):
-            out_ref[n * (step // BLK) + j, 0] = part[:, j * BLK : (j + 1) * BLK]
+    count = out_ref.shape[0] * out_ref.shape[1]
+    part = times(held_ref[:, :depth], own_ref[...]) + times(held_ref[:, depth:], other_ref[...])
+    part = part.astype(BF)
+    for j in range(count):
+        out_ref[j % out_ref.shape[0], j // out_ref.shape[0]] = part[:, j * BLK : (j + 1) * BLK]
 
 
 def columns_product(which_core, low, own, other, n_x, n_zh):
     n_ab, many, wide = low.shape
     out_rows, depth = own.shape
-    block = pl.BlockSpec((out_rows // n_zh, depth), lambda n: (n, 0))
+    steps = 2
+    block = pl.BlockSpec((out_rows // steps, depth), lambda n: (n, 0))
     return pl.pallas_call(
         columns_kernel,
-        grid=(n_zh,),
+        grid=(steps,),
         out_shape=shape(n_x, n_zh, many, wide),
         in_specs=[SMEM, pl.BlockSpec((n_ab, many, wide), lambda n: (0, 0, 0)), block, block],
-        out_specs=pl.BlockSpec((n_x, 1, many, wide), lambda n: (0, n, 0, 0)),
+        out_specs=pl.BlockSpec((n_x, n_zh // steps, many, wide), lambda n: (0, n, 0, 0)),
         scratch_shapes=[pltpu.VMEM((many, 2 * depth), BF)],
         compiler_params=pltpu.CompilerParams(vmem_limit_bytes=LARGE),
         cost_estimate=pl.CostEstimate(flops=2 << 30, bytes_accessed=7 * MIB, transcendentals=0),
@@ -256,6 +256,30 @@
     for i in range(1, ref.shape[0]):
         total = total + ref[i].astype(F32)
     return total
+
+
+def gather_sum_kernel(parts_hbm, out_ref, parts_ref, sems):
+    copies = []
+    for j in range(out_ref.shape[0]):
+        copies.append(pltpu.make_async_copy(parts_hbm.at[:, j], parts_ref.at[:, j], sems.at[j]))
+        copies[-1].start()
+    for j in range(out_ref.shape[0]):
+        copies[j].wait()
+        total = parts_ref[0, j].astype(F32)
+        for i in range(1, parts_ref.shape[0]):
+            total = total + parts_ref[i, j].astype(F32)
+        out_ref[j] = total.astype(BF)
+
+
+def sum_sources(parts):
+    return pl.pallas_call(
+        gather_sum_kernel,
+        out_shape=shape(*parts.shape[1:]),
+        in_specs=[ANY],
+        out_specs=VMEM,
+        scratch_shapes=[pltpu.VMEM(parts.shape, BF), pltpu.SemaphoreType.DMA((parts.shape[1],))],
+        compiler_params=pltpu.CompilerParams(vmem_limit_bytes=WHOLE),
+    )(parts)
 
 
 def swap_rows(values, diagonal):
@@ -418,8 +442,7 @@
         pass_on(j, send[j - 1])
     part, slots[1::2], send = lax.optimization_barrier((part, slots[1::2], send))
 
-    part = jnp.sum(part.astype(F32), axis=0).astype(BF)
-    part = lax.all_to_all(part, "zh", 0, 0, tiled=True)
+    part = lax.all_to_all(sum_sources(part), "zh", 0, 0, tiled=True)
     for j in range(2, n_ab, 2):
         pass_on(j, send[j - 1])
     part, slots[2::2] = lax.optimization_barrier((part, slots[2::2]))

time: 176 us -> 169 us (0.960)
  local copies, waits for them, and re-layouts: 7.02 us -> 2.1 us
  other arithmetic: 5.5 us -> 2.95 us
  starting transfers between devices: 52.9 us -> 50.9 us
  Pallas kernels: 26.4 us -> 28.3 us
    unnamed x30 -> x18, local copies, waits for them, and re-layouts: 5.61 us -> 0.7 us
    all_to_all x2 -> x1, starting transfers between devices: 7.16 us -> 3.38 us  [body(): part = lax.all_to_all(part, 'zh', 0, 0, tiled=True)]
    all_to_all x0 -> x1, starting transfers between devices: none -> 3.47 us  [body(): part = lax.all_to_all(sum_sources(part), 'zh', 0, 0, tiled=True)]
    reduce_sum x1 -> x0, other arithmetic: 2.54 us -> none  [body(): part = jnp.sum(part.astype(F32), axis=0).astype(BF)]
    all_to_all x1, waiting for transfers between devices: 3.86 us -> 5.8 us  [body(): lax.all_to_all(jnp.broadcast_to(start[None], (n_ab, many, wide)), AB, 0,...]
    all_to_all x2 -> x1, waiting for transfers between devices: 10.2 us -> 8.65 us  [body(): part = lax.all_to_all(part, 'zh', 0, 0, tiled=True)]
    pallas_call x1 -> x2, Pallas kernels: 5.79 us -> 6.99 us  [the longest x1 4.77 us: columns_product(): pl.pallas_call(columns_kernel, grid=(steps,), out_shape=shape(n_x, n_zh,...]
  transfers between devices with their start and end apart: 18 -> 18, of which waited for: 14 -> 14; matrix products, arithmetic and copies ran while one was open for 2% -> 2% of each run, Pallas kernels for 6% -> 7%
where the time goes in v3:
time: 169 us; the launch traced here: 168 us
  starting transfers between devices  50.9 us (30%)
  waiting for transfers between devices  47.5 us (28%)
  blocking collectives  35.6 us (21%)
  Pallas kernels  28.3 us (17%)
  other arithmetic  2.95 us (2%)
  local copies, waits for them, and re-layouts  2.1 us (1%)
    all_to_all x1, blocking collectives, body(): lax.all_to_all(pack.reshape(cells, rows, 2 * wide), GRID, 0, 0, tiled=True)  21.8 us
    all_to_all x1, starting transfers between devices, body(): low = lax.all_to_all(low, AB, 0, 0, tiled=True)  16.5 us
    all_to_all x1, blocking collectives, body(): part = lax.all_to_all(part, 'x', 0, 0, tiled=True)  13.9 us
    ppermute x7, waiting for transfers between devices, pass_on(): lax.ppermute(block, AB, [(k, (k + j) % n_ab) for k in range(n_ab)])  13 us
    pallas_call x7, Pallas kernels, call(): pl.pallas_call(kernel, out_shape=out_shape, in_specs=specs, out_specs=out...  9.21 us
    ppermute x7, starting transfers between devices, pass_on(): lax.ppermute(block, AB, [(k, (k + j) % n_ab) for k in range(n_ab)])  8.66 us
    all_to_all x1, waiting for transfers between devices, body(): part = lax.all_to_all(part, 'zh', 0, 0, tiled=True)  8.65 us
    all_to_all x1, starting transfers between devices, body(): part = lax.all_to_all(part, 'x', 0, 0, tiled=True)  7.17 us
  transfers between devices with their start and end apart: 18, of which 14 were waited for; matrix products, arithmetic and copies ran while one was open for 2% of the time, Pallas kernels for 7%

profile of v3, /device:TPU:2, one launch (start us, length us, event | category | flops | bytes accessed | tf_op | source)
XLA Modules:
  0.0 167.7 jit_solution(15889158336294978135)
XLA Ops:
  0.0 1.7 %shard_map.73 = bf16[4,4,24,256]{3,2,1,0:T(8,128)(2,1)} custom-call(f32[24,2048]{1,0:T(8,128)} %amplitudes_hbm.1, f32[24,2048]{1,0:T(8,128)} %driver_ref.1), custom_call_target="tpu_custom_call" | custom-call | tf_op jit(solution)/shard_map/pallas_call | solution.py:79
  1.7 21.8 %all_to_all.40 = bf16[16,24,256]{2,1,0:T(8,128)(2,1)S(1)} all-to-all(bf16[16,24,256]{2,1,0:T(8,128)(2,1)} %bitcast.16), channel_id=1, replica_groups=mesh['y'=4,'zl'=2,'zh'=4,'x'=4,'core'=2] {'x','zh'}, dimensions={0} | all-to-all | bytes 393216 | tf_op jit(solution)/shard_map/all_to_all | solution.py:388
  24.5 4.9 %all-to-all-start.1 = ((bf16[8,384,128]{2,1,0:T(8,128)(2,1)}), bf16[8,384,128]{2,1,0:T(8,128)(2,1)S(1)}, u32[]{:S(2)}, u32[]{:S(2)}) async-start(bf16[8,384,128]{2,1,0:T(8,128)(2,1)} %broadcast_in_dim.76), calls=%async_computation.1 | async-start | bytes 1572864 | tf_op jit(solution)/shard_map/all_to_all | solution.py:425
  30.7 5.0 %shard_map.74 = (bf16[2048,512]{1,0:T(8,128)(2,1)}, bf16[2048,512]{1,0:T(8,128)(2,1)}) custom-call(s32[4,16]{1,0:T(4,128)S(1)} %bitcast.14, s32[4,16]{1,0:T(4,128)S(1)} %collective-permute-done.1.other_mask_ref, bf16[2048,512]{1,0:T(8,128)(2,1)} %ladder_ref, bf16[2048,512]{1,0:T(8,128)(2,1)} %collective-permute-done.other_ref), custom_call_target="tpu_custom_call" | custom-call | flops 1048576 | bytes 8388608 | tf_op jit(solution)/shard_map/pallas_call | solution.py:103
  35.7 5.8 %all-to-all-done.1.low_ref = bf16[8,384,128]{2,1,0:T(8,128)(2,1)S(1)} async-done(((bf16[8,384,128]{2,1,0:T(8,128)(2,1)}), bf16[8,384,128]{2,1,0:T(8,128)(2,1)S(1)}, u32[]{:S(2)}, u32[]{:S(2)}) %all-to-all-start.1) | async-done | bytes 786464 | tf_op jit(solution)/shard_map/all_to_all | solution.py:425
  41.5 4.8 %shard_map.75 = bf16[4,4,384,128]{3,2,1,0:T(8,128)(2,1)} custom-call(s32[1]{0:T(128)} %bitcast.1.core_ref, bf16[8,384,128]{2,1,0:T(8,128)(2,1)S(1)} %all-to-all-done.1.low_ref, bf16[2048,512]{1,0:T(8,128)(2,1)} %get-tuple-element.63.own_ref.masked_ref, bf16[2048,512]{1,0:T(8,128)(2,1)} %get-tuple-element.64.other_ref), custom_call_target="tpu_custom_call" | custom-call | flops 2147483648 | bytes 7340032 | tf_op jit(solution)/shard_map/pallas_call | solution.py:197
  46.3 7.2 %all-to-all-start.2 = ((bf16[4,4,384,128]{3,2,1,0:T(8,128)(2,1)}), bf16[4,4,384,128]{3,2,1,0:T(8,128)(2,1)}, u32[]{:S(2)}, u32[]{:S(2)}) async-start(bf16[4,4,384,128]{3,2,1,0:T(8,128)(2,1)} %shard_map.75), calls=%async_computation.2 | async-start | bytes 3145728 | tf_op jit(solution)/shard_map/all_to_all | solution.py:428
  55.6 1.4 collective-permute-start.2
  58.0 2.0 %collective-permute-start.4 = (bf16[128,512]{1,0:T(8,128)(2,1)S(1)}, bf16[128,512]{1,0:T(8,128)(2,1)S(1)}, u32[]{:S(2)}, u32[]{:S(2)}) collective-permute-start(bf16[128,512]{1,0:T(8,128)(2,1)S(1)} %get-tuple-element.49), channel_id=1, source_target_pairs={{0,96},{32,128},{64,160},{96,192},{128,224},{160,0},{192,32},{224,... | collective-permute-start | bytes 393224 | tf_op jit(solution)/shard_map/ppermute | solution.py:439
  59.9 2.1 %collective-permute-start.5 = (bf16[128,512]{1,0:T(8,128)(2,1)S(1)}, bf16[128,512]{1,0:T(8,128)(2,1)S(1)}, u32[]{:S(2)}, u32[]{:S(2)}) collective-permute-start(bf16[128,512]{1,0:T(8,128)(2,1)S(1)} %get-tuple-element.50), channel_id=1, source_target_pairs={{0,32},{32,64},{64,96},{96,128},{128,160},{160,192},{192,224},{224... | collective-permute-start | bytes 393224 | tf_op jit(solution)/shard_map/ppermute | solution.py:439
  62.1 2.3 %collective-permute-done.3.refs_2_ = bf16[128,512]{1,0:T(8,128)(2,1)S(1)} collective-permute-done((bf16[128,512]{1,0:T(8,128)(2,1)S(1)}, bf16[128,512]{1,0:T(8,128)(2,1)S(1)}, u32[]{:S(2)}, u32[]{:S(2)}) %collective-permute-start.3) | collective-permute-done | bytes 131104 | tf_op jit(solution)/shard_map/ppermute | solution.py:439
  64.3 3.0 %collective-permute-done.4.refs_4_ = bf16[128,512]{1,0:T(8,128)(2,1)S(1)} collective-permute-done((bf16[128,512]{1,0:T(8,128)(2,1)S(1)}, bf16[128,512]{1,0:T(8,128)(2,1)S(1)}, u32[]{:S(2)}, u32[]{:S(2)}) %collective-permute-start.4) | collective-permute-done | bytes 131104 | tf_op jit(solution)/shard_map/ppermute | solution.py:439
  68.3 3.0 %all-to-all-done.2.parts_hbm = bf16[4,4,384,128]{3,2,1,0:T(8,128)(2,1)} async-done(((bf16[4,4,384,128]{3,2,1,0:T(8,128)(2,1)}), bf16[4,4,384,128]{3,2,1,0:T(8,128)(2,1)}, u32[]{:S(2)}, u32[]{:S(2)}) %all-to-all-start.2) | async-done | bytes 1572896 | tf_op jit(solution)/shard_map/all_to_all | solution.py:428
  71.3 2.2 %shard_map.77 = bf16[4,384,128]{2,1,0:T(8,128)(2,1)} custom-call(bf16[4,4,384,128]{3,2,1,0:T(8,128)(2,1)} %all-to-all-done.2.parts_hbm), custom_call_target="tpu_custom_call" | custom-call | tf_op jit(solution)/shard_map/pallas_call | solution.py:275
  73.6 3.5 %all-to-all-start.3 = ((bf16[4,384,128]{2,1,0:T(8,128)(2,1)}), bf16[4,384,128]{2,1,0:T(8,128)(2,1)S(1)}, u32[]{:S(2)}, u32[]{:S(2)}) async-start(bf16[4,384,128]{2,1,0:T(8,128)(2,1)} %shard_map.77), calls=%async_computation.3 | async-start | bytes 786432 | tf_op jit(solution)/shard_map/all_to_all | solution.py:445
  77.2 1.3 select_reduce_fusion.1
  80.9 2.9 %collective-permute-done.6.refs_1_ = bf16[128,512]{1,0:T(8,128)(2,1)S(1)} collective-permute-done((bf16[128,512]{1,0:T(8,128)(2,1)}, bf16[128,512]{1,0:T(8,128)(2,1)S(1)}, u32[]{:S(2)}, u32[]{:S(2)}) %collective-permute-start.6) | collective-permute-done | bytes 131104 | tf_op jit(solution)/shard_map/ppermute | solution.py:439
  83.8 2.5 %collective-permute-done.7.refs_3_ = bf16[128,512]{1,0:T(8,128)(2,1)S(1)} collective-permute-done((bf16[128,512]{1,0:T(8,128)(2,1)}, bf16[128,512]{1,0:T(8,128)(2,1)S(1)}, u32[]{:S(2)}, u32[]{:S(2)}) %collective-permute-start.7) | collective-permute-done | bytes 131104 | tf_op jit(solution)/shard_map/ppermute | solution.py:439
  86.3 1.3 collective-permute-done.8.refs_5_
  89.6 1.5 collective-permute-start.10
  91.4 3.4 %collective-permute-done.10.cross_ref = bf16[192,128]{1,0:T(8,128)(2,1)S(1)} collective-permute-done((bf16[192,128]{1,0:T(8,128)(2,1)S(1)}, bf16[192,128]{1,0:T(8,128)(2,1)S(1)}, u32[]{:S(2)}, u32[]{:S(2)}) %collective-permute-start.10) | collective-permute-done | bytes 49184 | tf_op jit(solution)/shard_map/ppermute | solution.py:459
  94.8 1.1 shard_map.79
  95.9 16.5 %all-to-all-start.4 = ((bf16[8,384,128]{2,1,0:T(8,128)(2,1)}), bf16[8,384,128]{2,1,0:T(8,128)(2,1)S(1)}, u32[]{:S(2)}, u32[]{:S(2)}) async-start(bf16[8,384,128]{2,1,0:T(8,128)(2,1)} %shard_map.79), calls=%async_computation.4 | async-start | bytes 1572864 | tf_op jit(solution)/shard_map/all_to_all | solution.py:468
  112.8 4.5 %shard_map.80.keep_ref = bf16[1152,1024]{1,0:T(8,128)(2,1)} custom-call(s32[1]{0:T(128)} %bitcast.mine_ref, bf16[2048,512]{1,0:T(8,128)(2,1)} %get-tuple-element.63.own_ref.masked_ref, bf16[2048,512]{1,0:T(8,128)(2,1)} %get-tuple-element.64.other_ref), custom_call_target="tpu_custom_call" | custom-call | tf_op jit(solution)/shard_map/pallas_call | solution.py:33
  117.2 5.3 %all-to-all-done.4.low_ref = bf16[8,384,128]{2,1,0:T(8,128)(2,1)S(1)} async-done(((bf16[8,384,128]{2,1,0:T(8,128)(2,1)}), bf16[8,384,128]{2,1,0:T(8,128)(2,1)S(1)}, u32[]{:S(2)}, u32[]{:S(2)}) %all-to-all-start.4) | async-done | bytes 786464 | tf_op jit(solution)/shard_map/all_to_all | solution.py:468
  122.5 5.4 %shard_map.82 = bf16[4,96,1152]{2,1,0:T(8,128)(2,1)S(1)} custom-call(s32[1]{0:T(128)} %bitcast.1.core_ref, bf16[8,384,128]{2,1,0:T(8,128)(2,1)S(1)} %all-to-all-done.4.low_ref, s32[384,1]{1,0:T(8,128)S(1)} %fusion.8.diag_ref, bf16[1152,1024]{1,0:T(8,128)(2,1)} %shard_map.80.keep_ref, bf16[1152,512]{1,0:T(8,128)(2,1)} %copy-done.1, ...), custom_call_target="tpu_custom_call" | custom-call | flops 2147483648 | bytes 7340032 | tf_op jit(solution)/shard_map/pallas_call | solution.py:235
  128.0 13.9 %all_to_all.41 = bf16[4,96,1152]{2,1,0:T(8,128)(2,1)S(1)} all-to-all(bf16[4,96,1152]{2,1,0:T(8,128)(2,1)S(1)} %shard_map.82), channel_id=1, replica_groups=mesh['y'=4,'zl'=2,'zh'=4,'x'=4,'core'=2] {'x'}, dimensions={0} | all-to-all | bytes 1769472 | tf_op jit(solution)/shard_map/all_to_all | solution.py:471
  142.7 3.4 %all-to-all-start.6 = ((bf16[4,24,1152]{2,1,0:T(8,128)(2,1)}), bf16[4,24,1152]{2,1,0:T(8,128)(2,1)S(1)}, u32[]{:S(2)}, u32[]{:S(2)}) async-start(bf16[4,24,1152]{2,1,0:T(8,128)(2,1)} %bitcast.6), calls=%async_computation.6 | async-start | bytes 442368 | tf_op jit(solution)/shard_map/all_to_all | solution.py:473
  146.2 8.7 %all-to-all-done.6.pieces_ref = bf16[4,24,1152]{2,1,0:T(8,128)(2,1)S(1)} async-done(((bf16[4,24,1152]{2,1,0:T(8,128)(2,1)}), bf16[4,24,1152]{2,1,0:T(8,128)(2,1)S(1)}, u32[]{:S(2)}, u32[]{:S(2)}) %all-to-all-start.6) | async-done | bytes 221216 | tf_op jit(solution)/shard_map/all_to_all | solution.py:473
  155.5 4.3 %all-to-all-start.7 = ((bf16[8,24,128]{2,1,0:T(8,128)(2,1)}), bf16[8,24,128]{2,1,0:T(8,128)(2,1)S(1)}, u32[]{:S(2)}, u32[]{:S(2)}) async-start(bf16[8,24,128]{2,1,0:T(8,128)(2,1)} %get-tuple-element.74), calls=%async_computation.7 | async-start | bytes 98304 | tf_op jit(solution)/shard_map/all_to_all | solution.py:480
  160.0 6.1 %all-to-all-done.7.tiles_ref = bf16[8,24,128]{2,1,0:T(8,128)(2,1)S(1)} async-done(((bf16[8,24,128]{2,1,0:T(8,128)(2,1)}), bf16[8,24,128]{2,1,0:T(8,128)(2,1)S(1)}, u32[]{:S(2)}, u32[]{:S(2)}) %all-to-all-start.7) | async-done | bytes 49184 | tf_op jit(solution)/shard_map/all_to_all | solution.py:480
  166.1 1.6 shard_map.84
  (55 shorter events, 13.3 us)
Async XLA Ops:
  0.0 30.7 %collective-permute-start = (bf16[2048,512]{1,0:T(8,128)(2,1)}, bf16[2048,512]{1,0:T(8,128)(2,1)}, u32[]{:S(2)}, u32[]{:S(2)}) collective-permute-start(bf16[2048,512]{1,0:T(8,128)(2,1)} %ladder_ref), channel_id=1, source_target_pairs={{0,1},{1,0},{2,3},{3,2},{4,5},{5,4},{6,7},{7,6},{8,9},{9,8},{10,11... | collective-permute-start | bytes 6291464 | tf_op jit(solution)/shard_map/ppermute | solution.py:392
  1.7 27.7 %copy-start.3 = (s32[16,4]{0,1:T(4,128)S(1)}, s32[16,4]{0,1:T(4,128)}, u32[]{:S(2)}) copy-start(s32[16,4]{0,1:T(4,128)} %param.10) | copy-start | bytes 772
  24.5 17.0 %all-to-all-start.1 = ((bf16[8,384,128]{2,1,0:T(8,128)(2,1)}), bf16[8,384,128]{2,1,0:T(8,128)(2,1)S(1)}, u32[]{:S(2)}, u32[]{:S(2)}) async-start(bf16[8,384,128]{2,1,0:T(8,128)(2,1)} %broadcast_in_dim.76), calls=%async_computation.1 | async-start | bytes 1572864 | tf_op jit(solution)/shard_map/all_to_all | solution.py:425
  29.4 1.2 collective-permute-start.1
  46.3 7.2 %copy-start.6 = (s32[768]{0:T(1024)S(1)}, s32[768]{0:T(1024)}, u32[]{:S(2)}) copy-start(s32[768]{0:T(1024)} %param.11) | copy-start | bytes 9220
  46.3 7.5 %copy-start = (bf16[2048,512]{1,0:T(8,128)(2,1)S(1)}, bf16[2048,512]{1,0:T(8,128)(2,1)}, u32[]{:S(2)}) copy-start(bf16[2048,512]{1,0:T(8,128)(2,1)} %get-tuple-element.63.own_ref.masked_ref) | copy-start | bytes 6291460
  46.3 25.0 %all-to-all-start.2 = ((bf16[4,4,384,128]{3,2,1,0:T(8,128)(2,1)}), bf16[4,4,384,128]{3,2,1,0:T(8,128)(2,1)}, u32[]{:S(2)}, u32[]{:S(2)}) async-start(bf16[4,4,384,128]{3,2,1,0:T(8,128)(2,1)} %shard_map.75), calls=%async_computation.2 | async-start | bytes 3145728 | tf_op jit(solution)/shard_map/all_to_all | solution.py:428
  54.9 0.7 copy-start.4
  55.6 21.5 %copy-start.8 = (f32[32]{0:T(128)S(1)}, f32[32]{0:T(128)}, u32[]{:S(2)}) copy-start(f32[32]{0:T(128)} %param.12) | copy-start | bytes 388
  55.6 21.6 %copy-start.7 = (f32[128]{0:T(128)S(1)}, f32[128]{0:T(128)}, u32[]{:S(2)}) copy-start(f32[128]{0:T(128)} %param.13) | copy-start | bytes 1540
  55.6 24.4 %copy-start.5 = (bf16[128,512]{1,0:T(8,128)(2,1)S(1)}, bf16[128,512]{1,0:T(8,128)(2,1)}, u32[]{:S(2)}) copy-start(bf16[128,512]{1,0:T(8,128)(2,1)} %copy-done.4) | copy-start | bytes 393220
  55.6 6.5 %collective-permute-start.2 = (bf16[128,512]{1,0:T(8,128)(2,1)S(1)}, bf16[128,512]{1,0:T(8,128)(2,1)S(1)}, u32[]{:S(2)}, u32[]{:S(2)}) collective-permute-start(bf16[128,512]{1,0:T(8,128)(2,1)S(1)} %get-tuple-element.47), channel_id=1, source_target_pairs={{0,224},{32,0},{64,32},{96,64},{128,96},{160,128},{192,160},{224,1... | collective-permute-start | bytes 393224 | tf_op jit(solution)/shard_map/ppermute | solution.py:439
  57.0 7.3 %collective-permute-start.3 = (bf16[128,512]{1,0:T(8,128)(2,1)S(1)}, bf16[128,512]{1,0:T(8,128)(2,1)S(1)}, u32[]{:S(2)}, u32[]{:S(2)}) collective-permute-start(bf16[128,512]{1,0:T(8,128)(2,1)S(1)} %get-tuple-element.48), channel_id=1, source_target_pairs={{0,160},{32,192},{64,224},{96,0},{128,32},{160,64},{192,96},{224,1... | collective-permute-start | bytes 393224 | tf_op jit(solution)/shard_map/ppermute | solution.py:439
  58.0 9.4 %collective-permute-start.4 = (bf16[128,512]{1,0:T(8,128)(2,1)S(1)}, bf16[128,512]{1,0:T(8,128)(2,1)S(1)}, u32[]{:S(2)}, u32[]{:S(2)}) collective-permute-start(bf16[128,512]{1,0:T(8,128)(2,1)S(1)} %get-tuple-element.49), channel_id=1, source_target_pairs={{0,96},{32,128},{64,160},{96,192},{128,224},{160,0},{192,32},{224,... | collective-permute-start | bytes 393224 | tf_op jit(solution)/shard_map/ppermute | solution.py:439
  59.9 8.4 %collective-permute-start.5 = (bf16[128,512]{1,0:T(8,128)(2,1)S(1)}, bf16[128,512]{1,0:T(8,128)(2,1)S(1)}, u32[]{:S(2)}, u32[]{:S(2)}) collective-permute-start(bf16[128,512]{1,0:T(8,128)(2,1)S(1)} %get-tuple-element.50), channel_id=1, source_target_pairs={{0,32},{32,64},{64,96},{96,128},{128,160},{160,192},{192,224},{224... | collective-permute-start | bytes 393224 | tf_op jit(solution)/shard_map/ppermute | solution.py:439
  73.6 15.1 %all-to-all-start.3 = ((bf16[4,384,128]{2,1,0:T(8,128)(2,1)}), bf16[4,384,128]{2,1,0:T(8,128)(2,1)S(1)}, u32[]{:S(2)}, u32[]{:S(2)}) async-start(bf16[4,384,128]{2,1,0:T(8,128)(2,1)} %shard_map.77), calls=%async_computation.3 | async-start | bytes 786432 | tf_op jit(solution)/shard_map/all_to_all | solution.py:445
  78.6 5.2 %collective-permute-start.6 = (bf16[128,512]{1,0:T(8,128)(2,1)}, bf16[128,512]{1,0:T(8,128)(2,1)S(1)}, u32[]{:S(2)}, u32[]{:S(2)}) collective-permute-start(bf16[128,512]{1,0:T(8,128)(2,1)} %get-tuple-element.55), channel_id=1, source_target_pairs={{0,192},{32,224},{64,0},{96,32},{128,64},{160,96},{192,128},{224,1... | collective-permute-start | bytes 393224 | tf_op jit(solution)/shard_map/ppermute | solution.py:439
  79.5 6.8 %collective-permute-start.7 = (bf16[128,512]{1,0:T(8,128)(2,1)}, bf16[128,512]{1,0:T(8,128)(2,1)S(1)}, u32[]{:S(2)}, u32[]{:S(2)}) collective-permute-start(bf16[128,512]{1,0:T(8,128)(2,1)} %get-tuple-element.56), channel_id=1, source_target_pairs={{0,128},{32,160},{64,192},{96,224},{128,0},{160,32},{192,64},{224,... | collective-permute-start | bytes 393224 | tf_op jit(solution)/shard_map/ppermute | solution.py:439
  80.0 7.6 %collective-permute-start.8 = (bf16[128,512]{1,0:T(8,128)(2,1)S(1)}, bf16[128,512]{1,0:T(8,128)(2,1)S(1)}, u32[]{:S(2)}, u32[]{:S(2)}) collective-permute-start(bf16[128,512]{1,0:T(8,128)(2,1)S(1)} %copy-done.5), channel_id=1, source_target_pairs={{0,64},{32,96},{64,128},{96,160},{128,192},{160,224},{192,0},{224,... | collective-permute-start | bytes 393224 | tf_op jit(solution)/shard_map/ppermute | solution.py:439
  88.9 2.5 %collective-permute-start.9 = (bf16[192,128]{1,0:T(8,128)(2,1)S(1)}, bf16[192,128]{1,0:T(8,128)(2,1)S(1)}, u32[]{:S(2)}, u32[]{:S(2)}) collective-permute-start(bf16[192,128]{1,0:T(8,128)(2,1)S(1)} %get-tuple-element.60), channel_id=1, source_target_pairs={{0,0},{1,1},{2,2},{3,3},{4,32},{5,33},{6,34},{7,35},{8,64},{9,65},... | collective-permute-start | bytes 147464 | tf_op jit(solution)/shard_map/ppermute | solution.py:458
  89.6 5.2 %collective-permute-start.10 = (bf16[192,128]{1,0:T(8,128)(2,1)S(1)}, bf16[192,128]{1,0:T(8,128)(2,1)S(1)}, u32[]{:S(2)}, u32[]{:S(2)}) collective-permute-start(bf16[192,128]{1,0:T(8,128)(2,1)S(1)} %get-tuple-element.61), channel_id=1, source_target_pairs={{0,2},{1,3},{2,0},{3,1},{4,34},{5,35},{6,32},{7,33},{8,66},{9,67},... | collective-permute-start | bytes 147464 | tf_op jit(solution)/shard_map/ppermute | solution.py:459
  95.9 26.6 %all-to-all-start.4 = ((bf16[8,384,128]{2,1,0:T(8,128)(2,1)}), bf16[8,384,128]{2,1,0:T(8,128)(2,1)S(1)}, u32[]{:S(2)}, u32[]{:S(2)}) async-start(bf16[8,384,128]{2,1,0:T(8,128)(2,1)} %shard_map.79), calls=%async_computation.4 | async-start | bytes 1572864 | tf_op jit(solution)/shard_map/all_to_all | solution.py:468
  112.5 4.7 %copy-start.1 = (bf16[1152,512]{1,0:T(8,128)(2,1)}, bf16[1152,512]{1,0:T(8,128)(2,1)S(1)}, u32[]{:S(2)}) copy-start(bf16[1152,512]{1,0:T(8,128)(2,1)S(1)} %shard_map.81.mown_ref) | copy-start | bytes 3538948
  112.5 4.7 %collective-permute-start.11 = (bf16[1152,512]{1,0:T(8,128)(2,1)S(1)}, bf16[1152,512]{1,0:T(8,128)(2,1)}, u32[]{:S(2)}, u32[]{:S(2)}) collective-permute-start(bf16[1152,512]{1,0:T(8,128)(2,1)S(1)} %shard_map.81.mown_ref), channel_id=1, source_target_pairs={{0,1},{1,0},{2,3},{3,2},{4,5},{5,4},{6,7},{7,6},{8,9},{9,8},{10,11... | collective-permute-start | bytes 3538952 | tf_op jit(solution)/shard_map/ppermute | solution.py:450
  127.9 38.2 %copy-start.2 = (f32[24,2048]{1,0:T(8,128)S(1)}, f32[24,2048]{1,0:T(8,128)}, u32[]{:S(2)}) copy-start(f32[24,2048]{1,0:T(8,128)} %driver_ref.1) | copy-start | bytes 589828
  142.7 12.2 %all-to-all-start.6 = ((bf16[4,24,1152]{2,1,0:T(8,128)(2,1)}), bf16[4,24,1152]{2,1,0:T(8,128)(2,1)S(1)}, u32[]{:S(2)}, u32[]{:S(2)}) async-start(bf16[4,24,1152]{2,1,0:T(8,128)(2,1)} %bitcast.6), calls=%async_computation.6 | async-start | bytes 442368 | tf_op jit(solution)/shard_map/all_to_all | solution.py:473
  155.5 10.6 %all-to-all-start.7 = ((bf16[8,24,128]{2,1,0:T(8,128)(2,1)}), bf16[8,24,128]{2,1,0:T(8,128)(2,1)S(1)}, u32[]{:S(2)}, u32[]{:S(2)}) async-start(bf16[8,24,128]{2,1,0:T(8,128)(2,1)} %get-tuple-element.74), calls=%async_computation.7 | async-start | bytes 98304 | tf_op jit(solution)/shard_map/all_to_all | solution.py:480

commit v4 on v3

--- a/solution.py
+++ b/solution.py
@@ -259,16 +259,19 @@
 
 
 def gather_sum_kernel(parts_hbm, out_ref, parts_ref, sems):
+    pieces, rows, _ = out_ref.shape
+    step = rows // 2
+    chunks = [(j, slice(i * step, (i + 1) * step)) for j in range(pieces) for i in range(2)]
     copies = []
-    for j in range(out_ref.shape[0]):
-        copies.append(pltpu.make_async_copy(parts_hbm.at[:, j], parts_ref.at[:, j], sems.at[j]))
+    for n, (j, here) in enumerate(chunks):
+        copies.append(pltpu.make_async_copy(parts_hbm.at[:, j, here], parts_ref.at[:, j, here], sems.at[n]))
         copies[-1].start()
-    for j in range(out_ref.shape[0]):
-        copies[j].wait()
-        total = parts_ref[0, j].astype(F32)
+    for n, (j, here) in enumerate(chunks):
+        copies[n].wait()
+        total = parts_ref[0, j, here].astype(F32)
         for i in range(1, parts_ref.shape[0]):
-            total = total + parts_ref[i, j].astype(F32)
-        out_ref[j] = total.astype(BF)
+            total = total + parts_ref[i, j, here].astype(F32)
+        out_ref[j, here] = total.astype(BF)
 
 
 def sum_sources(parts):
@@ -277,7 +280,7 @@
         out_shape=shape(*parts.shape[1:]),
         in_specs=[ANY],
         out_specs=VMEM,
-        scratch_shapes=[pltpu.VMEM(parts.shape, BF), pltpu.SemaphoreType.DMA((parts.shape[1],))],
+        scratch_shapes=[pltpu.VMEM(parts.shape, BF), pltpu.SemaphoreType.DMA((2 * parts.shape[1],))],
         compiler_params=pltpu.CompilerParams(vmem_limit_bytes=WHOLE),
     )(parts)
 
@@ -343,7 +346,7 @@
     count, _, half = tiles_ref.shape
     area = 2 * half
     lane, out = iotas(area, area)
-    turn = (lane == turned(out)).astype(F32)
+    turn = ones_where(lane == turned(out))
     for j in range(count):
         b = lax.rem(mine + j, count)
         if j == 0:
@@ -351,12 +354,10 @@
         else:
             own = total_ref[:, (j - 1) * half : j * half]
             theirs = swap_rows(tiles_ref[b].astype(F32), diag_ref[...])
-            behind = jnp.dot(
-                jnp.concatenate([theirs, own], axis=1),
-                turn,
-                precision=lax.Precision.HIGHEST,
-                preferred_element_type=F32,
-            )
+            both = jnp.concatenate([theirs, own], axis=1)
+            high = both.astype(BF)
+            behind = jnp.dot(high, turn, preferred_element_type=F32)
+            behind = behind + jnp.dot((both - high.astype(F32)).astype(BF), turn, preferred_element_type=F32)
             symmetric = jnp.where(mine < b, jnp.concatenate([own, theirs], axis=1), behind)
         here = pl.ds(pl.multiple_of(b * area, area), area)
         den = col_ref[:, here] - row_ref[...]
@@ -438,14 +439,20 @@
     def pass_on(j, block):
         slots[n_ab - j] = lax.ppermute(block, AB, [(k, (k + j) % n_ab) for k in range(n_ab)])
 
-    for j in range(1, n_ab, 2):
+    early = [j for j in range(1, n_ab) if j % 2 or 2 * j == n_ab]
+    for j in early:
         pass_on(j, send[j - 1])
-    part, slots[1::2], send = lax.optimization_barrier((part, slots[1::2], send))
+    part, arrived, send = lax.optimization_barrier((part, [slots[n_ab - j] for j in early], send))
+    for j, block in zip(early, arrived):
+        slots[n_ab - j] = block
 
     part = lax.all_to_all(sum_sources(part), "zh", 0, 0, tiled=True)
-    for j in range(2, n_ab, 2):
+    late = [j for j in range(1, n_ab) if j not in early]
+    for j in late:
         pass_on(j, send[j - 1])
-    part, slots[2::2] = lax.optimization_barrier((part, slots[2::2]))
+    part, arrived = lax.optimization_barrier((part, [slots[n_ab - j] for j in late]))
+    for j, block in zip(late, arrived):
+        slots[n_ab - j] = block
     mirror = call(join_kernel, shape(kept, in_cols), slots[1:] + [turn])
     mirror_other = lax.ppermute(mirror, "core", swap_core)
 

time: 169 us -> 167 us (0.988)
  waiting for transfers between devices: 47.5 us -> 45.5 us
    ppermute x7, waiting for transfers between devices: 13 us -> 8.09 us  [pass_on(): lax.ppermute(block, AB, [(k, (k + j) % n_ab) for k in range(n_ab)])]
    all_to_all x1, waiting for transfers between devices: 1.11 us -> 3.71 us  [body(): part = lax.all_to_all(sum_sources(part), 'zh', 0, 0, tiled=True)]
where the time goes in v4:
time: 167 us; the launch traced here: 166 us
  starting transfers between devices  52.3 us (31%)
  waiting for transfers between devices  45.5 us (27%)
  blocking collectives  34.9 us (21%)
  Pallas kernels  27.9 us (17%)
  other arithmetic  2.95 us (2%)
  local copies, waits for them, and re-layouts  2.08 us (1%)
    all_to_all x1, blocking collectives, body(): lax.all_to_all(pack.reshape(cells, rows, 2 * wide), GRID, 0, 0, tiled=True)  21.8 us
    all_to_all x1, starting transfers between devices, body(): low = lax.all_to_all(low, AB, 0, 0, tiled=True)  14.8 us
    all_to_all x1, blocking collectives, body(): part = lax.all_to_all(part, 'x', 0, 0, tiled=True)  13.1 us
    ppermute x7, starting transfers between devices, pass_on(): lax.ppermute(block, AB, [(k, (k + j) % n_ab) for k in range(n_ab)])  10.3 us
    all_to_all x1, waiting for transfers between devices, body(): part = lax.all_to_all(part, 'zh', 0, 0, tiled=True)  8.7 us
    pallas_call x7, Pallas kernels, call(): pl.pallas_call(kernel, out_shape=out_shape, in_specs=specs, out_specs=out...  8.64 us
    ppermute x7, waiting for transfers between devices, pass_on(): lax.ppermute(block, AB, [(k, (k + j) % n_ab) for k in range(n_ab)])  8.09 us
    all_to_all x1, starting transfers between devices, body(): part = lax.all_to_all(part, 'x', 0, 0, tiled=True)  7.17 us
  transfers between devices with their start and end apart: 18, of which 14 were waited for; matrix products, arithmetic and copies ran while one was open for 2% of the time, Pallas kernels for 7%

profile of v4, /device:TPU:2, one launch (start us, length us, event | category | flops | bytes accessed | tf_op | source)
XLA Modules:
  0.0 165.9 jit_solution(5311746620211999365)
XLA Ops:
  0.0 1.7 %shard_map.73 = bf16[4,4,24,256]{3,2,1,0:T(8,128)(2,1)} custom-call(f32[24,2048]{1,0:T(8,128)} %amplitudes_hbm.1, f32[24,2048]{1,0:T(8,128)} %driver_ref.1), custom_call_target="tpu_custom_call" | custom-call | tf_op jit(solution)/shard_map/pallas_call | solution.py:79
  1.7 21.8 %all_to_all.40 = bf16[16,24,256]{2,1,0:T(8,128)(2,1)S(1)} all-to-all(bf16[16,24,256]{2,1,0:T(8,128)(2,1)} %bitcast.16), channel_id=1, replica_groups=mesh['y'=4,'zl'=2,'zh'=4,'x'=4,'core'=2] {'x','zh'}, dimensions={0} | all-to-all | bytes 393216 | tf_op jit(solution)/shard_map/all_to_all | solution.py:389
  24.5 4.9 %all-to-all-start.1 = ((bf16[8,384,128]{2,1,0:T(8,128)(2,1)}), bf16[8,384,128]{2,1,0:T(8,128)(2,1)S(1)}, u32[]{:S(2)}, u32[]{:S(2)}) async-start(bf16[8,384,128]{2,1,0:T(8,128)(2,1)} %broadcast_in_dim.76), calls=%async_computation.1 | async-start | bytes 1572864 | tf_op jit(solution)/shard_map/all_to_all | solution.py:426
  29.6 1.1 collective-permute-done.1.other_mask_ref
  30.7 5.0 %shard_map.74 = (bf16[2048,512]{1,0:T(8,128)(2,1)}, bf16[2048,512]{1,0:T(8,128)(2,1)}) custom-call(s32[4,16]{1,0:T(4,128)S(1)} %bitcast.14, s32[4,16]{1,0:T(4,128)S(1)} %collective-permute-done.1.other_mask_ref, bf16[2048,512]{1,0:T(8,128)(2,1)} %ladder_ref, bf16[2048,512]{1,0:T(8,128)(2,1)} %collective-permute-done.other_ref), custom_call_target="tpu_custom_call" | custom-call | flops 1048576 | bytes 8388608 | tf_op jit(solution)/shard_map/pallas_call | solution.py:103
  35.7 5.8 %all-to-all-done.1.low_ref = bf16[8,384,128]{2,1,0:T(8,128)(2,1)S(1)} async-done(((bf16[8,384,128]{2,1,0:T(8,128)(2,1)}), bf16[8,384,128]{2,1,0:T(8,128)(2,1)S(1)}, u32[]{:S(2)}, u32[]{:S(2)}) %all-to-all-start.1) | async-done | bytes 786464 | tf_op jit(solution)/shard_map/all_to_all | solution.py:426
  41.5 4.8 %shard_map.75 = bf16[4,4,384,128]{3,2,1,0:T(8,128)(2,1)} custom-call(s32[1]{0:T(128)} %bitcast.1.core_ref, bf16[8,384,128]{2,1,0:T(8,128)(2,1)S(1)} %all-to-all-done.1.low_ref, bf16[2048,512]{1,0:T(8,128)(2,1)} %get-tuple-element.61.own_ref.masked_ref, bf16[2048,512]{1,0:T(8,128)(2,1)} %get-tuple-element.62.other_ref), custom_call_target="tpu_custom_call" | custom-call | flops 2147483648 | bytes 7340032 | tf_op jit(solution)/shard_map/pallas_call | solution.py:197
  46.3 7.2 %all-to-all-start.2 = ((bf16[4,4,384,128]{3,2,1,0:T(8,128)(2,1)}), bf16[4,4,384,128]{3,2,1,0:T(8,128)(2,1)}, u32[]{:S(2)}, u32[]{:S(2)}) async-start(bf16[4,4,384,128]{3,2,1,0:T(8,128)(2,1)} %shard_map.75), calls=%async_computation.2 | async-start | bytes 3145728 | tf_op jit(solution)/shard_map/all_to_all | solution.py:429
  57.2 3.8 %collective-permute-start.4 = (bf16[128,512]{1,0:T(8,128)(2,1)S(1)}, bf16[128,512]{1,0:T(8,128)(2,1)S(1)}, u32[]{:S(2)}, u32[]{:S(2)}) collective-permute-start(bf16[128,512]{1,0:T(8,128)(2,1)S(1)} %get-tuple-element.48), channel_id=1, source_target_pairs={{0,128},{32,160},{64,192},{96,224},{128,0},{160,32},{192,64},{224,... | collective-permute-start | bytes 393224 | tf_op jit(solution)/shard_map/ppermute | solution.py:440
  61.3 1.2 collective-permute-start.6
  62.5 1.9 %collective-permute-done.2.refs_6_ = bf16[128,512]{1,0:T(8,128)(2,1)S(1)} collective-permute-done((bf16[128,512]{1,0:T(8,128)(2,1)S(1)}, bf16[128,512]{1,0:T(8,128)(2,1)S(1)}, u32[]{:S(2)}, u32[]{:S(2)}) %collective-permute-start.2) | collective-permute-done | bytes 131104 | tf_op jit(solution)/shard_map/ppermute | solution.py:440
  64.4 1.5 collective-permute-done.3.refs_4_
  67.6 3.8 %all-to-all-done.2.parts_hbm = bf16[4,4,384,128]{3,2,1,0:T(8,128)(2,1)} async-done(((bf16[4,4,384,128]{3,2,1,0:T(8,128)(2,1)}), bf16[4,4,384,128]{3,2,1,0:T(8,128)(2,1)}, u32[]{:S(2)}, u32[]{:S(2)}) %all-to-all-start.2) | async-done | bytes 1572896 | tf_op jit(solution)/shard_map/all_to_all | solution.py:429
  71.3 2.3 %shard_map.77 = bf16[4,384,128]{2,1,0:T(8,128)(2,1)} custom-call(bf16[4,4,384,128]{3,2,1,0:T(8,128)(2,1)} %all-to-all-done.2.parts_hbm), custom_call_target="tpu_custom_call" | custom-call | tf_op jit(solution)/shard_map/pallas_call | solution.py:278
  73.7 3.5 %all-to-all-start.3 = ((bf16[4,384,128]{2,1,0:T(8,128)(2,1)}), bf16[4,384,128]{2,1,0:T(8,128)(2,1)S(1)}, u32[]{:S(2)}, u32[]{:S(2)}) async-start(bf16[4,384,128]{2,1,0:T(8,128)(2,1)} %shard_map.77), calls=%async_computation.3 | async-start | bytes 786432 | tf_op jit(solution)/shard_map/all_to_all | solution.py:449
  77.3 1.3 select_reduce_fusion.1
  78.7 3.2 %collective-permute-start.8 = (bf16[128,512]{1,0:T(8,128)(2,1)S(1)}, bf16[128,512]{1,0:T(8,128)(2,1)S(1)}, u32[]{:S(2)}, u32[]{:S(2)}) collective-permute-start(bf16[128,512]{1,0:T(8,128)(2,1)S(1)} %copy-done.5), channel_id=1, source_target_pairs={{0,192},{32,224},{64,0},{96,32},{128,64},{160,96},{192,128},{224,1... | collective-permute-start | bytes 393224 | tf_op jit(solution)/shard_map/ppermute | solution.py:440
  82.1 3.0 %collective-permute-done.7.refs_5_ = bf16[128,512]{1,0:T(8,128)(2,1)S(1)} collective-permute-done((bf16[128,512]{1,0:T(8,128)(2,1)}, bf16[128,512]{1,0:T(8,128)(2,1)S(1)}, u32[]{:S(2)}, u32[]{:S(2)}) %collective-permute-start.7) | collective-permute-done | bytes 131104 | tf_op jit(solution)/shard_map/ppermute | solution.py:440
  85.1 3.7 %all-to-all-done.3.pieces_ref = bf16[4,384,128]{2,1,0:T(8,128)(2,1)S(1)} async-done(((bf16[4,384,128]{2,1,0:T(8,128)(2,1)}), bf16[4,384,128]{2,1,0:T(8,128)(2,1)S(1)}, u32[]{:S(2)}, u32[]{:S(2)}) %all-to-all-start.3) | async-done | bytes 393248 | tf_op jit(solution)/shard_map/all_to_all | solution.py:449
  89.7 1.5 collective-permute-start.10
  91.5 2.8 %collective-permute-done.10.cross_ref = bf16[192,128]{1,0:T(8,128)(2,1)S(1)} collective-permute-done((bf16[192,128]{1,0:T(8,128)(2,1)S(1)}, bf16[192,128]{1,0:T(8,128)(2,1)S(1)}, u32[]{:S(2)}, u32[]{:S(2)}) %collective-permute-start.10) | collective-permute-done | bytes 49184 | tf_op jit(solution)/shard_map/ppermute | solution.py:466
  94.4 1.1 shard_map.79
  95.5 14.8 %all-to-all-start.4 = ((bf16[8,384,128]{2,1,0:T(8,128)(2,1)}), bf16[8,384,128]{2,1,0:T(8,128)(2,1)S(1)}, u32[]{:S(2)}, u32[]{:S(2)}) async-start(bf16[8,384,128]{2,1,0:T(8,128)(2,1)} %shard_map.79), calls=%async_computation.4 | async-start | bytes 1572864 | tf_op jit(solution)/shard_map/all_to_all | solution.py:475
  110.7 4.4 %shard_map.80.keep_ref = bf16[1152,1024]{1,0:T(8,128)(2,1)} custom-call(s32[1]{0:T(128)} %bitcast.mine_ref, bf16[2048,512]{1,0:T(8,128)(2,1)} %get-tuple-element.61.own_ref.masked_ref, bf16[2048,512]{1,0:T(8,128)(2,1)} %get-tuple-element.62.other_ref), custom_call_target="tpu_custom_call" | custom-call | tf_op jit(solution)/shard_map/pallas_call | solution.py:33
  115.1 5.3 %all-to-all-done.4.low_ref = bf16[8,384,128]{2,1,0:T(8,128)(2,1)S(1)} async-done(((bf16[8,384,128]{2,1,0:T(8,128)(2,1)}), bf16[8,384,128]{2,1,0:T(8,128)(2,1)S(1)}, u32[]{:S(2)}, u32[]{:S(2)}) %all-to-all-start.4) | async-done | bytes 786464 | tf_op jit(solution)/shard_map/all_to_all | solution.py:475
  120.5 5.4 %shard_map.82 = bf16[4,96,1152]{2,1,0:T(8,128)(2,1)S(1)} custom-call(s32[1]{0:T(128)} %bitcast.1.core_ref, bf16[8,384,128]{2,1,0:T(8,128)(2,1)S(1)} %all-to-all-done.4.low_ref, s32[384,1]{1,0:T(8,128)S(1)} %fusion.8.diag_ref, bf16[1152,1024]{1,0:T(8,128)(2,1)} %shard_map.80.keep_ref, bf16[1152,512]{1,0:T(8,128)(2,1)} %copy-done.1, ...), custom_call_target="tpu_custom_call" | custom-call | flops 2147483648 | bytes 7340032 | tf_op jit(solution)/shard_map/pallas_call | solution.py:235
  125.9 13.1 %all_to_all.41 = bf16[4,96,1152]{2,1,0:T(8,128)(2,1)S(1)} all-to-all(bf16[4,96,1152]{2,1,0:T(8,128)(2,1)S(1)} %shard_map.82), channel_id=1, replica_groups=mesh['y'=4,'zl'=2,'zh'=4,'x'=4,'core'=2] {'x'}, dimensions={0} | all-to-all | bytes 1769472 | tf_op jit(solution)/shard_map/all_to_all | solution.py:478
  139.8 4.8 %all-to-all-start.6 = ((bf16[4,24,1152]{2,1,0:T(8,128)(2,1)}), bf16[4,24,1152]{2,1,0:T(8,128)(2,1)S(1)}, u32[]{:S(2)}, u32[]{:S(2)}) async-start(bf16[4,24,1152]{2,1,0:T(8,128)(2,1)} %bitcast.6), calls=%async_computation.6 | async-start | bytes 442368 | tf_op jit(solution)/shard_map/all_to_all | solution.py:480
  144.8 8.7 %all-to-all-done.6.pieces_ref = bf16[4,24,1152]{2,1,0:T(8,128)(2,1)S(1)} async-done(((bf16[4,24,1152]{2,1,0:T(8,128)(2,1)}), bf16[4,24,1152]{2,1,0:T(8,128)(2,1)S(1)}, u32[]{:S(2)}, u32[]{:S(2)}) %all-to-all-start.6) | async-done | bytes 221216 | tf_op jit(solution)/shard_map/all_to_all | solution.py:480
  154.2 4.3 %all-to-all-start.7 = ((bf16[8,24,128]{2,1,0:T(8,128)(2,1)}), bf16[8,24,128]{2,1,0:T(8,128)(2,1)S(1)}, u32[]{:S(2)}, u32[]{:S(2)}) async-start(bf16[8,24,128]{2,1,0:T(8,128)(2,1)} %get-tuple-element.72), calls=%async_computation.7 | async-start | bytes 98304 | tf_op jit(solution)/shard_map/all_to_all | solution.py:487
  158.6 6.1 %all-to-all-done.7.tiles_ref = bf16[8,24,128]{2,1,0:T(8,128)(2,1)S(1)} async-done(((bf16[8,24,128]{2,1,0:T(8,128)(2,1)}), bf16[8,24,128]{2,1,0:T(8,128)(2,1)S(1)}, u32[]{:S(2)}, u32[]{:S(2)}) %all-to-all-start.7) | async-done | bytes 49184 | tf_op jit(solution)/shard_map/all_to_all | solution.py:487
  164.7 1.1 shard_map.84
  (55 shorter events, 10.4 us)
Async XLA Ops:
  0.0 30.7 %collective-permute-start = (bf16[2048,512]{1,0:T(8,128)(2,1)}, bf16[2048,512]{1,0:T(8,128)(2,1)}, u32[]{:S(2)}, u32[]{:S(2)}) collective-permute-start(bf16[2048,512]{1,0:T(8,128)(2,1)} %ladder_ref), channel_id=1, source_target_pairs={{0,1},{1,0},{2,3},{3,2},{4,5},{5,4},{6,7},{7,6},{8,9},{9,8},{10,11... | collective-permute-start | bytes 6291464 | tf_op jit(solution)/shard_map/ppermute | solution.py:393
  1.7 27.7 %copy-start.3 = (s32[16,4]{0,1:T(4,128)S(1)}, s32[16,4]{0,1:T(4,128)}, u32[]{:S(2)}) copy-start(s32[16,4]{0,1:T(4,128)} %param.10) | copy-start | bytes 772
  24.5 17.0 %all-to-all-start.1 = ((bf16[8,384,128]{2,1,0:T(8,128)(2,1)}), bf16[8,384,128]{2,1,0:T(8,128)(2,1)S(1)}, u32[]{:S(2)}, u32[]{:S(2)}) async-start(bf16[8,384,128]{2,1,0:T(8,128)(2,1)} %broadcast_in_dim.76), calls=%async_computation.1 | async-start | bytes 1572864 | tf_op jit(solution)/shard_map/all_to_all | solution.py:426
  29.4 1.2 collective-permute-start.1
  46.3 7.2 %copy-start.6 = (s32[768]{0:T(1024)S(1)}, s32[768]{0:T(1024)}, u32[]{:S(2)}) copy-start(s32[768]{0:T(1024)} %param.11) | copy-start | bytes 9220
  46.3 7.5 %copy-start = (bf16[2048,512]{1,0:T(8,128)(2,1)S(1)}, bf16[2048,512]{1,0:T(8,128)(2,1)}, u32[]{:S(2)}) copy-start(bf16[2048,512]{1,0:T(8,128)(2,1)} %get-tuple-element.61.own_ref.masked_ref) | copy-start | bytes 6291460
  46.3 25.0 %all-to-all-start.2 = ((bf16[4,4,384,128]{3,2,1,0:T(8,128)(2,1)}), bf16[4,4,384,128]{3,2,1,0:T(8,128)(2,1)}, u32[]{:S(2)}, u32[]{:S(2)}) async-start(bf16[4,4,384,128]{3,2,1,0:T(8,128)(2,1)} %shard_map.75), calls=%async_computation.2 | async-start | bytes 3145728 | tf_op jit(solution)/shard_map/all_to_all | solution.py:429
  54.8 0.7 copy-start.4
  55.4 21.7 %copy-start.8 = (f32[32]{0:T(128)S(1)}, f32[32]{0:T(128)}, u32[]{:S(2)}) copy-start(f32[32]{0:T(128)} %param.12) | copy-start | bytes 388
  55.4 21.9 %copy-start.7 = (f32[128]{0:T(128)S(1)}, f32[128]{0:T(128)}, u32[]{:S(2)}) copy-start(f32[128]{0:T(128)} %param.13) | copy-start | bytes 1540
  55.4 23.3 %copy-start.5 = (bf16[128,512]{1,0:T(8,128)(2,1)S(1)}, bf16[128,512]{1,0:T(8,128)(2,1)}, u32[]{:S(2)}) copy-start(bf16[128,512]{1,0:T(8,128)(2,1)} %copy-done.4) | copy-start | bytes 393220
  55.4 9.0 %collective-permute-start.2 = (bf16[128,512]{1,0:T(8,128)(2,1)S(1)}, bf16[128,512]{1,0:T(8,128)(2,1)S(1)}, u32[]{:S(2)}, u32[]{:S(2)}) collective-permute-start(bf16[128,512]{1,0:T(8,128)(2,1)S(1)} %get-tuple-element.46), channel_id=1, source_target_pairs={{0,32},{32,64},{64,96},{96,128},{128,160},{160,192},{192,224},{224... | collective-permute-start | bytes 393224 | tf_op jit(solution)/shard_map/ppermute | solution.py:440
  56.3 9.7 %collective-permute-start.3 = (bf16[128,512]{1,0:T(8,128)(2,1)S(1)}, bf16[128,512]{1,0:T(8,128)(2,1)S(1)}, u32[]{:S(2)}, u32[]{:S(2)}) collective-permute-start(bf16[128,512]{1,0:T(8,128)(2,1)S(1)} %get-tuple-element.47), channel_id=1, source_target_pairs={{0,96},{32,128},{64,160},{96,192},{128,224},{160,0},{192,32},{224,... | collective-permute-start | bytes 393224 | tf_op jit(solution)/shard_map/ppermute | solution.py:440
  57.2 9.2 %collective-permute-start.4 = (bf16[128,512]{1,0:T(8,128)(2,1)S(1)}, bf16[128,512]{1,0:T(8,128)(2,1)S(1)}, u32[]{:S(2)}, u32[]{:S(2)}) collective-permute-start(bf16[128,512]{1,0:T(8,128)(2,1)S(1)} %get-tuple-element.48), channel_id=1, source_target_pairs={{0,128},{32,160},{64,192},{96,224},{128,0},{160,32},{192,64},{224,... | collective-permute-start | bytes 393224 | tf_op jit(solution)/shard_map/ppermute | solution.py:440
  61.0 5.9 %collective-permute-start.5 = (bf16[128,512]{1,0:T(8,128)(2,1)S(1)}, bf16[128,512]{1,0:T(8,128)(2,1)S(1)}, u32[]{:S(2)}, u32[]{:S(2)}) collective-permute-start(bf16[128,512]{1,0:T(8,128)(2,1)S(1)} %get-tuple-element.49), channel_id=1, source_target_pairs={{0,160},{32,192},{64,224},{96,0},{128,32},{160,64},{192,96},{224,1... | collective-permute-start | bytes 393224 | tf_op jit(solution)/shard_map/ppermute | solution.py:440
  61.3 6.3 %collective-permute-start.6 = (bf16[128,512]{1,0:T(8,128)(2,1)S(1)}, bf16[128,512]{1,0:T(8,128)(2,1)S(1)}, u32[]{:S(2)}, u32[]{:S(2)}) collective-permute-start(bf16[128,512]{1,0:T(8,128)(2,1)S(1)} %get-tuple-element.50), channel_id=1, source_target_pairs={{0,224},{32,0},{64,32},{96,64},{128,96},{160,128},{192,160},{224,1... | collective-permute-start | bytes 393224 | tf_op jit(solution)/shard_map/ppermute | solution.py:440
  73.7 15.1 %all-to-all-start.3 = ((bf16[4,384,128]{2,1,0:T(8,128)(2,1)}), bf16[4,384,128]{2,1,0:T(8,128)(2,1)S(1)}, u32[]{:S(2)}, u32[]{:S(2)}) async-start(bf16[4,384,128]{2,1,0:T(8,128)(2,1)} %shard_map.77), calls=%async_computation.3 | async-start | bytes 786432 | tf_op jit(solution)/shard_map/all_to_all | solution.py:449
  78.7 6.4 %collective-permute-start.7 = (bf16[128,512]{1,0:T(8,128)(2,1)}, bf16[128,512]{1,0:T(8,128)(2,1)S(1)}, u32[]{:S(2)}, u32[]{:S(2)}) collective-permute-start(bf16[128,512]{1,0:T(8,128)(2,1)} %get-tuple-element.54), channel_id=1, source_target_pairs={{0,64},{32,96},{64,128},{96,160},{128,192},{160,224},{192,0},{224,... | collective-permute-start | bytes 393224 | tf_op jit(solution)/shard_map/ppermute | solution.py:440
  78.7 6.4 %collective-permute-start.8 = (bf16[128,512]{1,0:T(8,128)(2,1)S(1)}, bf16[128,512]{1,0:T(8,128)(2,1)S(1)}, u32[]{:S(2)}, u32[]{:S(2)}) collective-permute-start(bf16[128,512]{1,0:T(8,128)(2,1)S(1)} %copy-done.5), channel_id=1, source_target_pairs={{0,192},{32,224},{64,0},{96,32},{128,64},{160,96},{192,128},{224,1... | collective-permute-start | bytes 393224 | tf_op jit(solution)/shard_map/ppermute | solution.py:440
  89.0 2.5 %collective-permute-start.9 = (bf16[192,128]{1,0:T(8,128)(2,1)S(1)}, bf16[192,128]{1,0:T(8,128)(2,1)S(1)}, u32[]{:S(2)}, u32[]{:S(2)}) collective-permute-start(bf16[192,128]{1,0:T(8,128)(2,1)S(1)} %get-tuple-element.58), channel_id=1, source_target_pairs={{0,0},{1,1},{2,2},{3,3},{4,32},{5,33},{6,34},{7,35},{8,64},{9,65},... | collective-permute-start | bytes 147464 | tf_op jit(solution)/shard_map/ppermute | solution.py:465
  89.7 4.6 %collective-permute-start.10 = (bf16[192,128]{1,0:T(8,128)(2,1)S(1)}, bf16[192,128]{1,0:T(8,128)(2,1)S(1)}, u32[]{:S(2)}, u32[]{:S(2)}) collective-permute-start(bf16[192,128]{1,0:T(8,128)(2,1)S(1)} %get-tuple-element.59), channel_id=1, source_target_pairs={{0,2},{1,3},{2,0},{3,1},{4,34},{5,35},{6,32},{7,33},{8,66},{9,67},... | collective-permute-start | bytes 147464 | tf_op jit(solution)/shard_map/ppermute | solution.py:466
  95.5 25.0 %all-to-all-start.4 = ((bf16[8,384,128]{2,1,0:T(8,128)(2,1)}), bf16[8,384,128]{2,1,0:T(8,128)(2,1)S(1)}, u32[]{:S(2)}, u32[]{:S(2)}) async-start(bf16[8,384,128]{2,1,0:T(8,128)(2,1)} %shard_map.79), calls=%async_computation.4 | async-start | bytes 1572864 | tf_op jit(solution)/shard_map/all_to_all | solution.py:475
  110.4 4.7 %copy-start.1 = (bf16[1152,512]{1,0:T(8,128)(2,1)}, bf16[1152,512]{1,0:T(8,128)(2,1)S(1)}, u32[]{:S(2)}) copy-start(bf16[1152,512]{1,0:T(8,128)(2,1)S(1)} %shard_map.81.mown_ref) | copy-start | bytes 3538948
  110.4 4.7 %collective-permute-start.11 = (bf16[1152,512]{1,0:T(8,128)(2,1)S(1)}, bf16[1152,512]{1,0:T(8,128)(2,1)}, u32[]{:S(2)}, u32[]{:S(2)}) collective-permute-start(bf16[1152,512]{1,0:T(8,128)(2,1)S(1)} %shard_map.81.mown_ref), channel_id=1, source_target_pairs={{0,1},{1,0},{2,3},{3,2},{4,5},{5,4},{6,7},{7,6},{8,9},{9,8},{10,11... | collective-permute-start | bytes 3538952 | tf_op jit(solution)/shard_map/ppermute | solution.py:457
  125.9 38.9 %copy-start.2 = (f32[24,2048]{1,0:T(8,128)S(1)}, f32[24,2048]{1,0:T(8,128)}, u32[]{:S(2)}) copy-start(f32[24,2048]{1,0:T(8,128)} %driver_ref.1) | copy-start | bytes 589828
  139.8 13.7 %all-to-all-start.6 = ((bf16[4,24,1152]{2,1,0:T(8,128)(2,1)}), bf16[4,24,1152]{2,1,0:T(8,128)(2,1)S(1)}, u32[]{:S(2)}, u32[]{:S(2)}) async-start(bf16[4,24,1152]{2,1,0:T(8,128)(2,1)} %bitcast.6), calls=%async_computation.6 | async-start | bytes 442368 | tf_op jit(solution)/shard_map/all_to_all | solution.py:480
  154.2 10.6 %all-to-all-start.7 = ((bf16[8,24,128]{2,1,0:T(8,128)(2,1)}), bf16[8,24,128]{2,1,0:T(8,128)(2,1)S(1)}, u32[]{:S(2)}, u32[]{:S(2)}) async-start(bf16[8,24,128]{2,1,0:T(8,128)(2,1)} %get-tuple-element.72), calls=%async_computation.7 | async-start | bytes 98304 | tf_op jit(solution)/shard_map/all_to_all | solution.py:487

commit v5 on v4

--- a/solution.py
+++ b/solution.py
@@ -442,11 +442,12 @@
     early = [j for j in range(1, n_ab) if j % 2 or 2 * j == n_ab]
     for j in early:
         pass_on(j, send[j - 1])
+    part = sum_sources(part)
     part, arrived, send = lax.optimization_barrier((part, [slots[n_ab - j] for j in early], send))
     for j, block in zip(early, arrived):
         slots[n_ab - j] = block
 
-    part = lax.all_to_all(sum_sources(part), "zh", 0, 0, tiled=True)
+    part = lax.all_to_all(part, "zh", 0, 0, tiled=True)
     late = [j for j in range(1, n_ab) if j not in early]
     for j in late:
         pass_on(j, send[j - 1])

time: 167 us -> 167 us (level)
    ppermute x7, waiting for transfers between devices: 8.09 us -> 3.05 us  [pass_on(): lax.ppermute(block, AB, [(k, (k + j) % n_ab) for k in range(n_ab)])]
    all_to_all x1, waiting for transfers between devices: 3.76 us -> 8.7 us  [body(): part = lax.all_to_all(part, 'x', 0, 0, tiled=True)]
    all_to_all x1 -> x2, waiting for transfers between devices: 8.7 us -> 12.4 us  [body(): part = lax.all_to_all(part, 'zh', 0, 0, tiled=True)]
    all_to_all x1 -> x0, waiting for transfers between devices: 3.71 us -> none  [body(): part = lax.all_to_all(sum_sources(part), 'zh', 0, 0, tiled=True)]
    all_to_all x1 -> x0, starting transfers between devices: 3.47 us -> none  [body(): part = lax.all_to_all(sum_sources(part), 'zh', 0, 0, tiled=True)]
    all_to_all x1 -> x2, starting transfers between devices: 4.82 us -> 8.28 us  [body(): part = lax.all_to_all(part, 'zh', 0, 0, tiled=True)]
  transfers between devices with their start and end apart: 18 -> 18, of which waited for: 14 -> 9; matrix products, arithmetic and copies ran while one was open for 2% -> 2% of each run, Pallas kernels for 7% -> 9%
where the time goes in v5:
time: 167 us; the launch traced here: 166 us
  starting transfers between devices  52.3 us (31%)
  waiting for transfers between devices  45.4 us (27%)
  blocking collectives  34.9 us (21%)
  Pallas kernels  28 us (17%)
  other arithmetic  2.95 us (2%)
  local copies, waits for them, and re-layouts  2.1 us (1%)
    all_to_all x1, blocking collectives, body(): lax.all_to_all(pack.reshape(cells, rows, 2 * wide), GRID, 0, 0, tiled=True)  21.8 us
    all_to_all x1, starting transfers between devices, body(): low = lax.all_to_all(low, AB, 0, 0, tiled=True)  14.8 us
    all_to_all x1, blocking collectives, body(): part = lax.all_to_all(part, 'x', 0, 0, tiled=True)  13.1 us
    all_to_all x2, waiting for transfers between devices, body(): part = lax.all_to_all(part, 'zh', 0, 0, tiled=True)  12.4 us
    ppermute x7, starting transfers between devices, pass_on(): lax.ppermute(block, AB, [(k, (k + j) % n_ab) for k in range(n_ab)])  10.3 us
    pallas_call x7, Pallas kernels, call(): pl.pallas_call(kernel, out_shape=out_shape, in_specs=specs, out_specs=out...  8.74 us
    all_to_all x1, waiting for transfers between devices, body(): part = lax.all_to_all(part, 'x', 0, 0, tiled=True)  8.7 us
    all_to_all x2, starting transfers between devices, body(): part = lax.all_to_all(part, 'zh', 0, 0, tiled=True)  8.28 us
  transfers between devices with their start and end apart: 18, of which 9 were waited for; matrix products, arithmetic and copies ran while one was open for 2% of the time, Pallas kernels for 9%

profile of v5, /device:TPU:2, one launch (start us, length us, event | category | flops | bytes accessed | tf_op | source)
XLA Modules:
  0.0 165.9 jit_solution(3479213336211940824)
XLA Ops:
  0.0 1.7 %shard_map.73 = bf16[4,4,24,256]{3,2,1,0:T(8,128)(2,1)} custom-call(f32[24,2048]{1,0:T(8,128)} %amplitudes_hbm.1, f32[24,2048]{1,0:T(8,128)} %driver_ref.1), custom_call_target="tpu_custom_call" | custom-call | tf_op jit(solution)/shard_map/pallas_call | solution.py:79
  1.7 21.8 %all_to_all.40 = bf16[16,24,256]{2,1,0:T(8,128)(2,1)S(1)} all-to-all(bf16[16,24,256]{2,1,0:T(8,128)(2,1)} %bitcast.16), channel_id=1, replica_groups=mesh['y'=4,'zl'=2,'zh'=4,'x'=4,'core'=2] {'x','zh'}, dimensions={0} | all-to-all | bytes 393216 | tf_op jit(solution)/shard_map/all_to_all | solution.py:389
  23.5 1.0 broadcast_in_dim.76
  24.5 4.9 %all-to-all-start.1 = ((bf16[8,384,128]{2,1,0:T(8,128)(2,1)}), bf16[8,384,128]{2,1,0:T(8,128)(2,1)S(1)}, u32[]{:S(2)}, u32[]{:S(2)}) async-start(bf16[8,384,128]{2,1,0:T(8,128)(2,1)} %broadcast_in_dim.76), calls=%async_computation.1 | async-start | bytes 1572864 | tf_op jit(solution)/shard_map/all_to_all | solution.py:426
  29.6 1.1 collective-permute-done.1.other_mask_ref
  30.7 5.0 %shard_map.74 = (bf16[2048,512]{1,0:T(8,128)(2,1)}, bf16[2048,512]{1,0:T(8,128)(2,1)}) custom-call(s32[4,16]{1,0:T(4,128)S(1)} %bitcast.14, s32[4,16]{1,0:T(4,128)S(1)} %collective-permute-done.1.other_mask_ref, bf16[2048,512]{1,0:T(8,128)(2,1)} %ladder_ref, bf16[2048,512]{1,0:T(8,128)(2,1)} %collective-permute-done.other_ref), custom_call_target="tpu_custom_call" | custom-call | flops 1048576 | bytes 8388608 | tf_op jit(solution)/shard_map/pallas_call | solution.py:103
  35.7 5.8 %all-to-all-done.1.low_ref = bf16[8,384,128]{2,1,0:T(8,128)(2,1)S(1)} async-done(((bf16[8,384,128]{2,1,0:T(8,128)(2,1)}), bf16[8,384,128]{2,1,0:T(8,128)(2,1)S(1)}, u32[]{:S(2)}, u32[]{:S(2)}) %all-to-all-start.1) | async-done | bytes 786464 | tf_op jit(solution)/shard_map/all_to_all | solution.py:426
  41.5 4.8 %shard_map.75 = bf16[4,4,384,128]{3,2,1,0:T(8,128)(2,1)} custom-call(s32[1]{0:T(128)} %bitcast.1.core_ref, bf16[8,384,128]{2,1,0:T(8,128)(2,1)S(1)} %all-to-all-done.1.low_ref, bf16[2048,512]{1,0:T(8,128)(2,1)} %get-tuple-element.61.own_ref.masked_ref, bf16[2048,512]{1,0:T(8,128)(2,1)} %get-tuple-element.62.other_ref), custom_call_target="tpu_custom_call" | custom-call | flops 2147483648 | bytes 7340032 | tf_op jit(solution)/shard_map/pallas_call | solution.py:197
  46.3 7.2 %all-to-all-start.2 = ((bf16[4,4,384,128]{3,2,1,0:T(8,128)(2,1)}), bf16[4,4,384,128]{3,2,1,0:T(8,128)(2,1)}, u32[]{:S(2)}, u32[]{:S(2)}) async-start(bf16[4,4,384,128]{3,2,1,0:T(8,128)(2,1)} %shard_map.75), calls=%async_computation.2 | async-start | bytes 3145728 | tf_op jit(solution)/shard_map/all_to_all | solution.py:429
  53.8 1.1 shard_map.77
  57.3 3.8 %collective-permute-start.4 = (bf16[128,512]{1,0:T(8,128)(2,1)}, bf16[128,512]{1,0:T(8,128)(2,1)S(1)}, u32[]{:S(2)}, u32[]{:S(2)}) collective-permute-start(bf16[128,512]{1,0:T(8,128)(2,1)} %get-tuple-element.48), channel_id=1, source_target_pairs={{0,128},{32,160},{64,192},{96,224},{128,0},{160,32},{192,64},{224,... | collective-permute-start | bytes 393224 | tf_op jit(solution)/shard_map/ppermute | solution.py:440
  61.4 1.2 collective-permute-start.6
  62.6 8.7 %all-to-all-done.2.parts_hbm = bf16[4,4,384,128]{3,2,1,0:T(8,128)(2,1)} async-done(((bf16[4,4,384,128]{3,2,1,0:T(8,128)(2,1)}), bf16[4,4,384,128]{3,2,1,0:T(8,128)(2,1)}, u32[]{:S(2)}, u32[]{:S(2)}) %all-to-all-start.2) | async-done | bytes 1572896 | tf_op jit(solution)/shard_map/all_to_all | solution.py:429
  71.3 2.3 %shard_map.76 = bf16[4,384,128]{2,1,0:T(8,128)(2,1)} custom-call(bf16[4,4,384,128]{3,2,1,0:T(8,128)(2,1)} %all-to-all-done.2.parts_hbm), custom_call_target="tpu_custom_call" | custom-call | tf_op jit(solution)/shard_map/pallas_call | solution.py:278
  73.7 3.5 %all-to-all-start.3 = ((bf16[4,384,128]{2,1,0:T(8,128)(2,1)}), bf16[4,384,128]{2,1,0:T(8,128)(2,1)S(1)}, u32[]{:S(2)}, u32[]{:S(2)}) async-start(bf16[4,384,128]{2,1,0:T(8,128)(2,1)} %shard_map.76), calls=%async_computation.3 | async-start | bytes 786432 | tf_op jit(solution)/shard_map/all_to_all | solution.py:450
  77.4 1.3 select_reduce_fusion.1
  78.8 3.2 %collective-permute-start.8 = (bf16[128,512]{1,0:T(8,128)(2,1)S(1)}, bf16[128,512]{1,0:T(8,128)(2,1)S(1)}, u32[]{:S(2)}, u32[]{:S(2)}) collective-permute-start(bf16[128,512]{1,0:T(8,128)(2,1)S(1)} %copy-done.5), channel_id=1, source_target_pairs={{0,192},{32,224},{64,0},{96,32},{128,64},{160,96},{192,128},{224,1... | collective-permute-start | bytes 393224 | tf_op jit(solution)/shard_map/ppermute | solution.py:440
  82.1 3.0 %collective-permute-done.7.refs_5_ = bf16[128,512]{1,0:T(8,128)(2,1)S(1)} collective-permute-done((bf16[128,512]{1,0:T(8,128)(2,1)}, bf16[128,512]{1,0:T(8,128)(2,1)S(1)}, u32[]{:S(2)}, u32[]{:S(2)}) %collective-permute-start.7) | collective-permute-done | bytes 131104 | tf_op jit(solution)/shard_map/ppermute | solution.py:440
  85.2 3.7 %all-to-all-done.3.pieces_ref = bf16[4,384,128]{2,1,0:T(8,128)(2,1)S(1)} async-done(((bf16[4,384,128]{2,1,0:T(8,128)(2,1)}), bf16[4,384,128]{2,1,0:T(8,128)(2,1)S(1)}, u32[]{:S(2)}, u32[]{:S(2)}) %all-to-all-start.3) | async-done | bytes 393248 | tf_op jit(solution)/shard_map/all_to_all | solution.py:450
  89.8 1.5 collective-permute-start.10
  91.6 2.8 %collective-permute-done.10.cross_ref = bf16[192,128]{1,0:T(8,128)(2,1)S(1)} collective-permute-done((bf16[192,128]{1,0:T(8,128)(2,1)S(1)}, bf16[192,128]{1,0:T(8,128)(2,1)S(1)}, u32[]{:S(2)}, u32[]{:S(2)}) %collective-permute-start.10) | collective-permute-done | bytes 49184 | tf_op jit(solution)/shard_map/ppermute | solution.py:467
  94.4 1.1 shard_map.79
  95.6 14.8 %all-to-all-start.4 = ((bf16[8,384,128]{2,1,0:T(8,128)(2,1)}), bf16[8,384,128]{2,1,0:T(8,128)(2,1)S(1)}, u32[]{:S(2)}, u32[]{:S(2)}) async-start(bf16[8,384,128]{2,1,0:T(8,128)(2,1)} %shard_map.79), calls=%async_computation.4 | async-start | bytes 1572864 | tf_op jit(solution)/shard_map/all_to_all | solution.py:476
  110.8 4.4 %shard_map.80.keep_ref = bf16[1152,1024]{1,0:T(8,128)(2,1)} custom-call(s32[1]{0:T(128)} %bitcast.mine_ref, bf16[2048,512]{1,0:T(8,128)(2,1)} %get-tuple-element.61.own_ref.masked_ref, bf16[2048,512]{1,0:T(8,128)(2,1)} %get-tuple-element.62.other_ref), custom_call_target="tpu_custom_call" | custom-call | tf_op jit(solution)/shard_map/pallas_call | solution.py:33
  115.2 5.3 %all-to-all-done.4.low_ref = bf16[8,384,128]{2,1,0:T(8,128)(2,1)S(1)} async-done(((bf16[8,384,128]{2,1,0:T(8,128)(2,1)}), bf16[8,384,128]{2,1,0:T(8,128)(2,1)S(1)}, u32[]{:S(2)}, u32[]{:S(2)}) %all-to-all-start.4) | async-done | bytes 786464 | tf_op jit(solution)/shard_map/all_to_all | solution.py:476
  120.5 5.4 %shard_map.82 = bf16[4,96,1152]{2,1,0:T(8,128)(2,1)S(1)} custom-call(s32[1]{0:T(128)} %bitcast.1.core_ref, bf16[8,384,128]{2,1,0:T(8,128)(2,1)S(1)} %all-to-all-done.4.low_ref, s32[384,1]{1,0:T(8,128)S(1)} %fusion.8.diag_ref, bf16[1152,1024]{1,0:T(8,128)(2,1)} %shard_map.80.keep_ref, bf16[1152,512]{1,0:T(8,128)(2,1)} %copy-done.1, ...), custom_call_target="tpu_custom_call" | custom-call | flops 2147483648 | bytes 7340032 | tf_op jit(solution)/shard_map/pallas_call | solution.py:235
  125.9 13.1 %all_to_all.41 = bf16[4,96,1152]{2,1,0:T(8,128)(2,1)S(1)} all-to-all(bf16[4,96,1152]{2,1,0:T(8,128)(2,1)S(1)} %shard_map.82), channel_id=1, replica_groups=mesh['y'=4,'zl'=2,'zh'=4,'x'=4,'core'=2] {'x'}, dimensions={0} | all-to-all | bytes 1769472 | tf_op jit(solution)/shard_map/all_to_all | solution.py:479
  139.9 4.8 %all-to-all-start.6 = ((bf16[4,24,1152]{2,1,0:T(8,128)(2,1)}), bf16[4,24,1152]{2,1,0:T(8,128)(2,1)S(1)}, u32[]{:S(2)}, u32[]{:S(2)}) async-start(bf16[4,24,1152]{2,1,0:T(8,128)(2,1)} %bitcast.6), calls=%async_computation.6 | async-start | bytes 442368 | tf_op jit(solution)/shard_map/all_to_all | solution.py:481
  144.9 8.7 %all-to-all-done.6.pieces_ref = bf16[4,24,1152]{2,1,0:T(8,128)(2,1)S(1)} async-done(((bf16[4,24,1152]{2,1,0:T(8,128)(2,1)}), bf16[4,24,1152]{2,1,0:T(8,128)(2,1)S(1)}, u32[]{:S(2)}, u32[]{:S(2)}) %all-to-all-start.6) | async-done | bytes 221216 | tf_op jit(solution)/shard_map/all_to_all | solution.py:481
  154.2 4.3 %all-to-all-start.7 = ((bf16[8,24,128]{2,1,0:T(8,128)(2,1)}), bf16[8,24,128]{2,1,0:T(8,128)(2,1)S(1)}, u32[]{:S(2)}, u32[]{:S(2)}) async-start(bf16[8,24,128]{2,1,0:T(8,128)(2,1)} %get-tuple-element.72), calls=%async_computation.7 | async-start | bytes 98304 | tf_op jit(solution)/shard_map/all_to_all | solution.py:488
  158.6 6.1 %all-to-all-done.7.tiles_ref = bf16[8,24,128]{2,1,0:T(8,128)(2,1)S(1)} async-done(((bf16[8,24,128]{2,1,0:T(8,128)(2,1)}), bf16[8,24,128]{2,1,0:T(8,128)(2,1)S(1)}, u32[]{:S(2)}, u32[]{:S(2)}) %all-to-all-start.7) | async-done | bytes 49184 | tf_op jit(solution)/shard_map/all_to_all | solution.py:488
  164.8 1.1 shard_map.84
  (55 shorter events, 6.8 us)
Async XLA Ops:
  0.0 30.7 %collective-permute-start = (bf16[2048,512]{1,0:T(8,128)(2,1)}, bf16[2048,512]{1,0:T(8,128)(2,1)}, u32[]{:S(2)}, u32[]{:S(2)}) collective-permute-start(bf16[2048,512]{1,0:T(8,128)(2,1)} %ladder_ref), channel_id=1, source_target_pairs={{0,1},{1,0},{2,3},{3,2},{4,5},{5,4},{6,7},{7,6},{8,9},{9,8},{10,11... | collective-permute-start | bytes 6291464 | tf_op jit(solution)/shard_map/ppermute | solution.py:393
  1.7 27.7 %copy-start.3 = (s32[16,4]{0,1:T(4,128)S(1)}, s32[16,4]{0,1:T(4,128)}, u32[]{:S(2)}) copy-start(s32[16,4]{0,1:T(4,128)} %param.10) | copy-start | bytes 772
  24.5 17.0 %all-to-all-start.1 = ((bf16[8,384,128]{2,1,0:T(8,128)(2,1)}), bf16[8,384,128]{2,1,0:T(8,128)(2,1)S(1)}, u32[]{:S(2)}, u32[]{:S(2)}) async-start(bf16[8,384,128]{2,1,0:T(8,128)(2,1)} %broadcast_in_dim.76), calls=%async_computation.1 | async-start | bytes 1572864 | tf_op jit(solution)/shard_map/all_to_all | solution.py:426
  29.4 1.2 collective-permute-start.1
  46.3 7.2 %copy-start.6 = (s32[768]{0:T(1024)S(1)}, s32[768]{0:T(1024)}, u32[]{:S(2)}) copy-start(s32[768]{0:T(1024)} %param.11) | copy-start | bytes 9220
  46.3 7.5 %copy-start = (bf16[2048,512]{1,0:T(8,128)(2,1)S(1)}, bf16[2048,512]{1,0:T(8,128)(2,1)}, u32[]{:S(2)}) copy-start(bf16[2048,512]{1,0:T(8,128)(2,1)} %get-tuple-element.61.own_ref.masked_ref) | copy-start | bytes 6291460
  46.3 25.0 %all-to-all-start.2 = ((bf16[4,4,384,128]{3,2,1,0:T(8,128)(2,1)}), bf16[4,4,384,128]{3,2,1,0:T(8,128)(2,1)}, u32[]{:S(2)}, u32[]{:S(2)}) async-start(bf16[4,4,384,128]{3,2,1,0:T(8,128)(2,1)} %shard_map.75), calls=%async_computation.2 | async-start | bytes 3145728 | tf_op jit(solution)/shard_map/all_to_all | solution.py:429
  54.9 0.7 copy-start.4
  55.6 21.7 %copy-start.8 = (f32[32]{0:T(128)S(1)}, f32[32]{0:T(128)}, u32[]{:S(2)}) copy-start(f32[32]{0:T(128)} %param.12) | copy-start | bytes 388
  55.6 21.8 %copy-start.7 = (f32[128]{0:T(128)S(1)}, f32[128]{0:T(128)}, u32[]{:S(2)}) copy-start(f32[128]{0:T(128)} %param.13) | copy-start | bytes 1540
  55.6 23.2 %copy-start.5 = (bf16[128,512]{1,0:T(8,128)(2,1)S(1)}, bf16[128,512]{1,0:T(8,128)(2,1)}, u32[]{:S(2)}) copy-start(bf16[128,512]{1,0:T(8,128)(2,1)} %copy-done.4) | copy-start | bytes 393220
  55.6 18.1 %collective-permute-start.2 = (bf16[128,512]{1,0:T(8,128)(2,1)}, bf16[128,512]{1,0:T(8,128)(2,1)S(1)}, u32[]{:S(2)}, u32[]{:S(2)}) collective-permute-start(bf16[128,512]{1,0:T(8,128)(2,1)} %get-tuple-element.46), channel_id=1, source_target_pairs={{0,32},{32,64},{64,96},{96,128},{128,160},{160,192},{192,224},{224... | collective-permute-start | bytes 393224 | tf_op jit(solution)/shard_map/ppermute | solution.py:440
  56.4 17.3 %collective-permute-start.3 = (bf16[128,512]{1,0:T(8,128)(2,1)}, bf16[128,512]{1,0:T(8,128)(2,1)S(1)}, u32[]{:S(2)}, u32[]{:S(2)}) collective-permute-start(bf16[128,512]{1,0:T(8,128)(2,1)} %get-tuple-element.47), channel_id=1, source_target_pairs={{0,96},{32,128},{64,160},{96,192},{128,224},{160,0},{192,32},{224,... | collective-permute-start | bytes 393224 | tf_op jit(solution)/shard_map/ppermute | solution.py:440
  57.3 16.4 %collective-permute-start.4 = (bf16[128,512]{1,0:T(8,128)(2,1)}, bf16[128,512]{1,0:T(8,128)(2,1)S(1)}, u32[]{:S(2)}, u32[]{:S(2)}) collective-permute-start(bf16[128,512]{1,0:T(8,128)(2,1)} %get-tuple-element.48), channel_id=1, source_target_pairs={{0,128},{32,160},{64,192},{96,224},{128,0},{160,32},{192,64},{224,... | collective-permute-start | bytes 393224 | tf_op jit(solution)/shard_map/ppermute | solution.py:440
  61.2 12.6 %collective-permute-start.5 = (bf16[128,512]{1,0:T(8,128)(2,1)S(1)}, bf16[128,512]{1,0:T(8,128)(2,1)S(1)}, u32[]{:S(2)}, u32[]{:S(2)}) collective-permute-start(bf16[128,512]{1,0:T(8,128)(2,1)S(1)} %get-tuple-element.49), channel_id=1, source_target_pairs={{0,160},{32,192},{64,224},{96,0},{128,32},{160,64},{192,96},{224,1... | collective-permute-start | bytes 393224 | tf_op jit(solution)/shard_map/ppermute | solution.py:440
  61.4 12.3 %collective-permute-start.6 = (bf16[128,512]{1,0:T(8,128)(2,1)S(1)}, bf16[128,512]{1,0:T(8,128)(2,1)S(1)}, u32[]{:S(2)}, u32[]{:S(2)}) collective-permute-start(bf16[128,512]{1,0:T(8,128)(2,1)S(1)} %get-tuple-element.50), channel_id=1, source_target_pairs={{0,224},{32,0},{64,32},{96,64},{128,96},{160,128},{192,160},{224,1... | collective-permute-start | bytes 393224 | tf_op jit(solution)/shard_map/ppermute | solution.py:440
  73.7 15.1 %all-to-all-start.3 = ((bf16[4,384,128]{2,1,0:T(8,128)(2,1)}), bf16[4,384,128]{2,1,0:T(8,128)(2,1)S(1)}, u32[]{:S(2)}, u32[]{:S(2)}) async-start(bf16[4,384,128]{2,1,0:T(8,128)(2,1)} %shard_map.76), calls=%async_computation.3 | async-start | bytes 786432 | tf_op jit(solution)/shard_map/all_to_all | solution.py:450
  78.8 6.4 %collective-permute-start.7 = (bf16[128,512]{1,0:T(8,128)(2,1)}, bf16[128,512]{1,0:T(8,128)(2,1)S(1)}, u32[]{:S(2)}, u32[]{:S(2)}) collective-permute-start(bf16[128,512]{1,0:T(8,128)(2,1)} %get-tuple-element.54), channel_id=1, source_target_pairs={{0,64},{32,96},{64,128},{96,160},{128,192},{160,224},{192,0},{224,... | collective-permute-start | bytes 393224 | tf_op jit(solution)/shard_map/ppermute | solution.py:440
  78.8 6.4 %collective-permute-start.8 = (bf16[128,512]{1,0:T(8,128)(2,1)S(1)}, bf16[128,512]{1,0:T(8,128)(2,1)S(1)}, u32[]{:S(2)}, u32[]{:S(2)}) collective-permute-start(bf16[128,512]{1,0:T(8,128)(2,1)S(1)} %copy-done.5), channel_id=1, source_target_pairs={{0,192},{32,224},{64,0},{96,32},{128,64},{160,96},{192,128},{224,1... | collective-permute-start | bytes 393224 | tf_op jit(solution)/shard_map/ppermute | solution.py:440
  89.1 2.5 %collective-permute-start.9 = (bf16[192,128]{1,0:T(8,128)(2,1)S(1)}, bf16[192,128]{1,0:T(8,128)(2,1)S(1)}, u32[]{:S(2)}, u32[]{:S(2)}) collective-permute-start(bf16[192,128]{1,0:T(8,128)(2,1)S(1)} %get-tuple-element.58), channel_id=1, source_target_pairs={{0,0},{1,1},{2,2},{3,3},{4,32},{5,33},{6,34},{7,35},{8,64},{9,65},... | collective-permute-start | bytes 147464 | tf_op jit(solution)/shard_map/ppermute | solution.py:466
  89.8 4.6 %collective-permute-start.10 = (bf16[192,128]{1,0:T(8,128)(2,1)S(1)}, bf16[192,128]{1,0:T(8,128)(2,1)S(1)}, u32[]{:S(2)}, u32[]{:S(2)}) collective-permute-start(bf16[192,128]{1,0:T(8,128)(2,1)S(1)} %get-tuple-element.59), channel_id=1, source_target_pairs={{0,2},{1,3},{2,0},{3,1},{4,34},{5,35},{6,32},{7,33},{8,66},{9,67},... | collective-permute-start | bytes 147464 | tf_op jit(solution)/shard_map/ppermute | solution.py:467
  95.6 25.0 %all-to-all-start.4 = ((bf16[8,384,128]{2,1,0:T(8,128)(2,1)}), bf16[8,384,128]{2,1,0:T(8,128)(2,1)S(1)}, u32[]{:S(2)}, u32[]{:S(2)}) async-start(bf16[8,384,128]{2,1,0:T(8,128)(2,1)} %shard_map.79), calls=%async_computation.4 | async-start | bytes 1572864 | tf_op jit(solution)/shard_map/all_to_all | solution.py:476
  110.5 4.7 %copy-start.1 = (bf16[1152,512]{1,0:T(8,128)(2,1)}, bf16[1152,512]{1,0:T(8,128)(2,1)S(1)}, u32[]{:S(2)}) copy-start(bf16[1152,512]{1,0:T(8,128)(2,1)S(1)} %shard_map.81.mown_ref) | copy-start | bytes 3538948
  110.5 4.7 %collective-permute-start.11 = (bf16[1152,512]{1,0:T(8,128)(2,1)S(1)}, bf16[1152,512]{1,0:T(8,128)(2,1)}, u32[]{:S(2)}, u32[]{:S(2)}) collective-permute-start(bf16[1152,512]{1,0:T(8,128)(2,1)S(1)} %shard_map.81.mown_ref), channel_id=1, source_target_pairs={{0,1},{1,0},{2,3},{3,2},{4,5},{5,4},{6,7},{7,6},{8,9},{9,8},{10,11... | collective-permute-start | bytes 3538952 | tf_op jit(solution)/shard_map/ppermute | solution.py:458
  125.9 38.9 %copy-start.2 = (f32[24,2048]{1,0:T(8,128)S(1)}, f32[24,2048]{1,0:T(8,128)}, u32[]{:S(2)}) copy-start(f32[24,2048]{1,0:T(8,128)} %driver_ref.1) | copy-start | bytes 589828
  139.9 13.7 %all-to-all-start.6 = ((bf16[4,24,1152]{2,1,0:T(8,128)(2,1)}), bf16[4,24,1152]{2,1,0:T(8,128)(2,1)S(1)}, u32[]{:S(2)}, u32[]{:S(2)}) async-start(bf16[4,24,1152]{2,1,0:T(8,128)(2,1)} %bitcast.6), calls=%async_computation.6 | async-start | bytes 442368 | tf_op jit(solution)/shard_map/all_to_all | solution.py:481
  154.2 10.6 %all-to-all-start.7 = ((bf16[8,24,128]{2,1,0:T(8,128)(2,1)}), bf16[8,24,128]{2,1,0:T(8,128)(2,1)S(1)}, u32[]{:S(2)}, u32[]{:S(2)}) async-start(bf16[8,24,128]{2,1,0:T(8,128)(2,1)} %get-tuple-element.72), calls=%async_computation.7 | async-start | bytes 98304 | tf_op jit(solution)/shard_map/all_to_all | solution.py:488
